TPU v7x, 32 devices: a whole 2x2x4 slice. The times are simulated.
32 devices in a mesh: groups: 2 (over y), row: 4 (over z), col: 2 (over x), sub: 2 (over core).
Axes of the slice: x: 2, y: 2, z: 4, core: 2. Of those that a mesh axis runs over, the one named last changes fastest.
Arguments:
- pulses: bfloat16 [2, 8, 2, 256, 1024], P(None, ('groups', 'row'), None, 'sub'), parts along dimension 1, may hold values from -6 to 6
- owner: int32 [4], P('groups'), parts along dimension 0, may hold values from 0 to 3
- centres: int32 [8, 2, 2], P(('groups', 'row'), 'col'), parts along dimension 0, may hold values from 0 to 31
Outputs:
- formed_image: float32 [256, 2, 512], P(('groups', 'row'), None, ('col', 'sub')), parts along dimension 0
- despeckled: float32 [256, 512], P(('groups', 'row'), ('col', 'sub')), parts along dimension 0
There are 2 independent parts, one for each index of `groups`. A program takes and returns all parts, laid end to end along the dimension named above; each array names one. Nothing has to cross between parts.
All inputs are finite; a program needn't handle non-finite values.
Results may differ from a plain program's by a relative error of at most 0.0068.
Values may be sent and summed in bfloat16 or wider, within the bound.
A program may use at most 64 MiB of HBM per device.

v0:
```python
import math

import jax
import jax.numpy as jnp
from jax import lax
from jax.sharding import PartitionSpec as P

F = 1024
PB = 256
NBLK = 2
TR = 32
TC = 128
RAD = 16


SIGMA_RANGE = 1.0
TWO_PI = 2.0 * math.pi


def from_root(block, axis, source):
    block = jnp.where(lax.axis_index(axis) == source, block, jnp.zeros_like(block))
    return lax.psum(block, axis)


def padded_2(block, sides, width):
    for axis, dim in sides:
        count = lax.axis_size(axis)
        forward = [(i, i + 1) for i in range(count - 1)]
        backward = [(target, source) for source, target in forward]
        low = lax.ppermute(
            lax.slice_in_dim(block, block.shape[dim] - width, None, axis=dim), axis, forward
        )
        high = lax.ppermute(lax.slice_in_dim(block, 0, width, axis=dim), axis, backward)
        block = jnp.concatenate([low, block, high], axis=dim)
    return block


def rephase(pulse_block, global_pulses, shift_rows, shift_cols, row_count):
    frequency = jnp.arange(F, dtype=jnp.int32)
    freq_index = frequency * shift_cols % F
    pulse_index = global_pulses * shift_rows % row_count
    phase_angle = TWO_PI * (
        freq_index.astype(jnp.float32)[None, :] / F
        + pulse_index.astype(jnp.float32)[:, None] / row_count
    )
    cosine = jnp.cos(phase_angle)
    sine_part = jnp.sin(phase_angle)
    real_part = pulse_block[0].astype(jnp.float32)
    imag_part = pulse_block[1].astype(jnp.float32)
    return (
        (real_part * cosine - imag_part * sine_part).astype(jnp.bfloat16),
        (real_part * sine_part + imag_part * cosine).astype(jnp.bfloat16),
    )


def range_table(global_cols):
    frequency = jnp.arange(F, dtype=jnp.int32)
    phase_index = frequency[:, None] * global_cols[None, :] % F
    phase_angle = TWO_PI * phase_index.astype(jnp.float32) / F
    norm_scale = 1.0 / math.sqrt(F)
    return jnp.concatenate(
        [
            (jnp.cos(phase_angle) * norm_scale).astype(jnp.bfloat16),
            (-jnp.sin(phase_angle) * norm_scale).astype(jnp.bfloat16),
        ],
        axis=1,
    )


def azimuth_table(global_rows, global_pulses, row_count):
    phase_index = global_rows[:, None] * global_pulses[None, :] % row_count
    phase_angle = TWO_PI * phase_index.astype(jnp.float32) / row_count
    norm_scale = 1.0 / math.sqrt(NBLK * PB)
    return jnp.concatenate(
        [
            (jnp.cos(phase_angle) * norm_scale).astype(jnp.bfloat16),
            (-jnp.sin(phase_angle) * norm_scale).astype(jnp.bfloat16),
        ],
        axis=1,
    )


def compress(rephased_real, rephased_imag, freq_table):
    pulse_count = rephased_real.shape[0]
    col_count = freq_table.shape[1] // 2
    operand = jnp.concatenate([rephased_real, rephased_imag], axis=0)
    product = jnp.dot(operand, freq_table, preferred_element_type=jnp.float32)
    comp_real = (product[:pulse_count, :col_count] - product[pulse_count:, col_count:]).astype(
        jnp.bfloat16
    )
    comp_imag = (product[:pulse_count, col_count:] + product[pulse_count:, :col_count]).astype(
        jnp.bfloat16
    )
    return (comp_real, comp_imag)


def form_block(
    pulse_block, global_pulses, global_rows, freq_table, shift_rows, shift_cols, row_count
):
    rephased_real, rephased_imag = rephase(
        pulse_block, global_pulses, shift_rows, shift_cols, row_count
    )
    comp_real, comp_imag = compress(rephased_real, rephased_imag, freq_table)
    az_table = azimuth_table(global_rows, global_pulses, row_count)
    stacked_rows = jnp.concatenate(
        [
            jnp.concatenate([comp_real, comp_imag], axis=1),
            jnp.concatenate([-comp_imag, comp_real], axis=1),
        ],
        axis=0,
    )
    return jnp.dot(az_table, stacked_rows, preferred_element_type=jnp.float32)


def bilateral(padded, row_inside, col_inside):
    height = padded.shape[0] - 2 * RAD
    breadth = padded.shape[1] - 2 * RAD
    center = padded[RAD : RAD + height, RAD : RAD + breadth]
    numerator = center
    weight = jnp.ones_like(center)
    for distance in range(1, RAD + 1):
        spatial = 2.0 * distance * distance / (RAD * RAD)
        for offset in (-distance, distance):
            row_near = padded[RAD + offset : RAD + offset + height, RAD : RAD + breadth]
            row_flag = row_inside[RAD + offset : RAD + offset + height][:, None]
            col_near = padded[RAD : RAD + height, RAD + offset : RAD + offset + breadth]
            col_flag = col_inside[RAD + offset : RAD + offset + breadth][None, :]
            for neighbour, inside in ((row_near, row_flag), (col_near, col_flag)):
                contrast = neighbour - center
                kernel = (
                    jnp.exp(-spatial - contrast * contrast * (0.5 / (SIGMA_RANGE * SIGMA_RANGE)))
                    * inside
                )
                numerator = numerator + kernel * neighbour
                weight = weight + kernel
    return numerator / weight


def per_device(pulses, owner, centres):
    n_rows = lax.axis_size("row")
    n_cols = lax.axis_size("col")
    n_subs = lax.axis_size("sub")
    row_id = lax.axis_index("row")
    col_id = lax.axis_index("col")
    sub_id = lax.axis_index("sub")
    all_rows = TR * n_rows
    all_cols = TC * n_cols * n_subs
    shift_rows = centres[0, 0, 0]
    shift_cols = centres[0, 0, 1]
    pulse_count = pulses.shape[3]
    global_rows = row_id * TR + jnp.arange(TR, dtype=jnp.int32)
    chip_cols = n_subs * TC
    global_cols = col_id * chip_cols + jnp.arange(chip_cols, dtype=jnp.int32)
    freq_table = range_table(global_cols)
    accumulated = jnp.zeros((TR, 2 * chip_cols), jnp.float32)
    for block_id in range(NBLK):
        received = from_root(pulses[block_id, 0], "row", owner[block_id])
        global_pulses = (
            block_id * PB + sub_id * pulse_count + jnp.arange(pulse_count, dtype=jnp.int32)
        )
        accumulated = accumulated + form_block(
            received, global_pulses, global_rows, freq_table, shift_rows, shift_cols, all_rows
        )
    own_image = lax.psum_scatter(
        accumulated.reshape(TR, 2, chip_cols), "sub", scatter_dimension=2, tiled=True
    )
    intensity = own_image[:, 0] * own_image[:, 0] + own_image[:, 1] * own_image[:, 1]
    col_start = (col_id * n_subs + sub_id) * TC
    row_glob = row_id * TR + jnp.arange(TR + 2 * RAD, dtype=jnp.int32) - RAD
    col_glob = col_start + jnp.arange(TC + 2 * RAD, dtype=jnp.int32) - RAD
    validity_row_inside = ((row_glob >= 0) & (row_glob < all_rows)).astype(jnp.float32)
    validity_col_inside = ((col_glob >= 0) & (col_glob < all_cols)).astype(jnp.float32)

    def smooth(field_values):
        padded = padded_2(field_values, (("row", 0), (("col", "sub"), 1)), RAD)
        return bilateral(padded, validity_row_inside, validity_col_inside)

    despeckled = smooth(smooth(intensity))
    return (own_image, despeckled)


def solution(mesh):
    return jax.shard_map(
        per_device,
        mesh=mesh,
        in_specs=(
            P(None, ("groups", "row"), None, "sub", None),
            P("groups"),
            P(("groups", "row"), "col", None),
        ),
        out_specs=(
            P(("groups", "row"), None, ("col", "sub")),
            P(("groups", "row"), ("col", "sub")),
        ),
        check_vma=False,
    )
```

profile of v0, /device:TPU:1, one launch (start us, length us, event | category | flops | bytes accessed | tf_op | source)
XLA Modules:
  0.0 138.5 jit_solution(17596479005384857318)
XLA Ops:
  7.2 1.3 fusion.184
  9.8 2.2 %select_bitcast_fusion = (bf16[2,128,1024]{2,1,0:T(8,128)(2,1)}, bf16[2,128,1024]{2,1,0:T(8,128)(2,1)}) fusion(bf16[2,1,2,128,1024]{4,3,2,1,0:T(8,128)(2,1)} %param.3, pred[]{:T(512)S(6)} %eq.18, pred[]{:T(512)S(6)} %eq.17), kind=kLoop, calls=%fused_computation.40 | loop fusion | flops 524288 | bytes 2097154 | tf_op jit(solution)/shard_map/jit(_where)/select_n | solution.py:21
  12.2 0.6 fusion.185
  12.8 0.7 fusion.163
  13.5 0.7 fusion.158
  14.2 0.2 multiply_convert_fusion.3
  14.5 4.5 %multiply_convert_fusion.1 = (bf16[1024,256]{1,0:T(8,128)(2,1)S(1)}, bf16[1024,256]{1,0:T(8,128)(2,1)S(1)}) fusion(s32[256]{0:T(256)S(1)} %iota_add_fusion), kind=kLoop, calls=%fused_computation.9 | loop fusion | flops 4980736 | bytes 1049600 | tf_op jit(solution)/shard_map/convert_element_type | solution.py:63
  19.0 47.8 %all-reduce.3.cloned.1.call-done = (bf16[2,128,1024]{2,1,0:T(8,128)(2,1)}, bf16[2,128,1024]{2,1,0:T(8,128)(2,1)}) async-done(((bf16[2,128,1024]{2,1,0:T(8,128)(2,1)}, bf16[2,128,1024]{2,1,0:T(8,128)(2,1)}), (bf16[2,128,1024]{2,1,0:T(8,128)(2,1)}, bf16[2,128,1024]{2,1,0:T(8,128)(2,1)})) %all-reduce.3.cloned.1.call-update) | async-done | bytes 1048592 | tf_op jit(solution)/shard_map/psum | solution.py:22
  66.7 6.2 %fusion.13 = (bf16[128,1024]{1,0:T(8,128)(2,1)S(1)}, bf16[128,1024]{1,0:T(8,128)(2,1)S(1)}, bf16[128,1024]{1,0:T(8,128)(2,1)S(1)}, bf16[128,1024]{1,0:T(8,128)(2,1)S(1)}) fusion(f32[128]{0:T(128)S(1)} %get-tuple-element.105, f32[1024]{0:T(1024)S(1)} %fusion.158, bf16[2,128,1024]{2,1,0:T(8,128)(2,1)} %get-tuple-element.3, ...), kind=kLoop, calls=%fused_computation.28 | loop fusion | flops 3145728 | bytes 2102272 | tf_op jit(solution)/shard_map/convert_element_type | solution.py:51
  73.0 0.4 fusion.7
  73.5 0.4 fusion.6
  74.0 0.1 fusion.26
  74.1 0.2 convolution_add_fusion
  74.3 4.4 %copy.7 = f32[32,2,256]{1,0,2:T(8,128)} copy(f32[32,2,256]{2,1,0:T(2,128)S(1)} %reshape.162) | data formatting | bytes 131072
  78.8 5.5 %reshape.167 = f32[256,64]{1,0:T(8,128)} reshape(f32[256,32,2]{2,1,0:T(8,128)} %bitcast.41) | data formatting | bytes 131072
  84.4 7.1 %reduce-scatter.4.cloned.1.call-done = f32[128,64]{1,0:T(8,128)} async-done(((f32[256,64]{1,0:T(8,128)}), f32[128,64]{1,0:T(8,128)}) %reduce-scatter.4.cloned.1.call-update) | async-done | bytes 32784
  91.5 3.0 %reshape.168 = f32[128,32,2]{2,1,0:T(8,128)S(1)} reshape(f32[128,64]{1,0:T(8,128)} %reduce-scatter.4.cloned.1.call-done) | data formatting | bytes 65536
  94.5 1.3 copy.8
  95.9 3.5 %collective-permute-start = (f32[16,128]{1,0:T(8,128)S(1)}, f32[16,128]{1,0:T(8,128)S(1)}, u32[]{:S(2)}, u32[]{:S(2)}) collective-permute-start(f32[16,128]{1,0:T(8,128)S(1)} %bitcast.47), channel_id=1, source_target_pairs={{0,4},{4,8},{8,12},{1,5},{5,9},{9,13},{2,6},{6,10},{10,14},{3,7},{... | collective-permute-start | bytes 24584 | tf_op jit(solution)/shard_map/ppermute | solution.py:30
  99.3 1.3 collective-permute-start.1
  100.7 3.0 %collective-permute-done.1 = f32[16,128]{1,0:T(8,128)S(1)} collective-permute-done((f32[16,128]{1,0:T(8,128)S(1)}, f32[16,128]{1,0:T(8,128)S(1)}, u32[]{:S(2)}, u32[]{:S(2)}) %collective-permute-start.1) | collective-permute-done | bytes 8224 | tf_op jit(solution)/shard_map/ppermute | solution.py:33
  103.8 4.6 %collective-permute-start.2 = (f32[64,16]{1,0:T(8,128)S(1)}, f32[64,16]{1,0:T(8,128)S(1)}, u32[]{:S(2)}, u32[]{:S(2)}) collective-permute-start(f32[64,16]{1,0:T(8,128)S(1)} %get-tuple-element.20), channel_id=1, source_target_pairs={{0,1},{1,2},{2,3},{4,5},{5,6},{6,7},{8,9},{9,10},{10,11},{12,13},{... | collective-permute-start | bytes 12296 | tf_op jit(solution)/shard_map/ppermute | solution.py:30
  108.4 1.9 %collective-permute-start.3 = (f32[64,16]{1,0:T(8,128)S(1)}, f32[64,16]{1,0:T(8,128)S(1)}, u32[]{:S(2)}, u32[]{:S(2)}) collective-permute-start(f32[64,16]{1,0:T(8,128)S(1)} %get-tuple-element.21), channel_id=1, source_target_pairs={{1,0},{2,1},{3,2},{5,4},{6,5},{7,6},{9,8},{10,9},{11,10},{13,12},{... | collective-permute-start | bytes 12296 | tf_op jit(solution)/shard_map/ppermute | solution.py:33
  110.4 3.2 %collective-permute-done.3 = f32[64,16]{1,0:T(8,128)S(1)} collective-permute-done((f32[64,16]{1,0:T(8,128)S(1)}, f32[64,16]{1,0:T(8,128)S(1)}, u32[]{:S(2)}, u32[]{:S(2)}) %collective-permute-start.3) | collective-permute-done | bytes 4128 | tf_op jit(solution)/shard_map/ppermute | solution.py:33
  113.7 0.5 fusion.134
  114.2 3.1 %collective-permute-start.4 = (f32[16,128]{1,0:T(8,128)S(1)}, f32[16,128]{1,0:T(8,128)S(1)}, u32[]{:S(2)}, u32[]{:S(2)}) collective-permute-start(f32[16,128]{1,0:T(8,128)S(1)} %get-tuple-element.22), channel_id=1, source_target_pairs={{0,4},{4,8},{8,12},{1,5},{5,9},{9,13},{2,6},{6,10},{10,14},{3,7},{... | collective-permute-start | bytes 24584 | tf_op jit(solution)/shard_map/ppermute | solution.py:30
  117.4 1.3 collective-permute-start.5
  118.7 3.1 %collective-permute-done.5 = f32[16,128]{1,0:T(8,128)S(1)} collective-permute-done((f32[16,128]{1,0:T(8,128)S(1)}, f32[16,128]{1,0:T(8,128)S(1)}, u32[]{:S(2)}, u32[]{:S(2)}) %collective-permute-start.5) | collective-permute-done | bytes 8224 | tf_op jit(solution)/shard_map/ppermute | solution.py:33
  121.8 3.3 %collective-permute-start.6 = (f32[64,16]{1,0:T(8,128)S(1)}, f32[64,16]{1,0:T(8,128)S(1)}, u32[]{:S(2)}, u32[]{:S(2)}) collective-permute-start(f32[64,16]{1,0:T(8,128)S(1)} %get-tuple-element.16), channel_id=1, source_target_pairs={{0,1},{1,2},{2,3},{4,5},{5,6},{6,7},{8,9},{9,10},{10,11},{12,13},{... | collective-permute-start | bytes 12296 | tf_op jit(solution)/shard_map/ppermute | solution.py:30
  125.2 1.9 %collective-permute-start.7 = (f32[64,16]{1,0:T(8,128)S(1)}, f32[64,16]{1,0:T(8,128)S(1)}, u32[]{:S(2)}, u32[]{:S(2)}) collective-permute-start(f32[64,16]{1,0:T(8,128)S(1)} %get-tuple-element.17), channel_id=1, source_target_pairs={{1,0},{2,1},{3,2},{5,4},{6,5},{7,6},{9,8},{10,9},{11,10},{13,12},{... | collective-permute-start | bytes 12296 | tf_op jit(solution)/shard_map/ppermute | solution.py:33
  127.1 3.3 %collective-permute-done.7 = f32[64,16]{1,0:T(8,128)S(1)} collective-permute-done((f32[64,16]{1,0:T(8,128)S(1)}, f32[64,16]{1,0:T(8,128)S(1)}, u32[]{:S(2)}, u32[]{:S(2)}) %collective-permute-start.7) | collective-permute-done | bytes 4128 | tf_op jit(solution)/shard_map/ppermute | solution.py:33
  130.5 1.2 fusion.115
  (35 shorter events, 1.0 us)
Async XLA Ops:
  7.2 5.0 %copy-start.1 = (s32[1,1,2]{2,1,0:T(1,128)S(1)}, s32[1,1,2]{2,1,0:T(1,128)}, u32[]{:S(2)}) copy-start(s32[1,1,2]{2,1,0:T(1,128)} %param.5) | copy-start | bytes 28
  7.2 59.6 %all-reduce.3.cloned.1.call-start = ((), (), s32[]{:S(2)}) async-start(), calls=%async_computation.2 | async-start | bytes 2097152 | tf_op jit(solution)/shard_map/psum | solution.py:22
  12.1 79.4 %reduce-scatter.4.cloned.1.call-start = ((), (), s32[]{:S(2)}) async-start(), calls=%async_computation.1 | async-start | bytes 196608
  95.8 35.9 %copy-start = (f32[32,2,128]{2,1,0:T(2,128)}, f32[32,2,128]{2,1,0:T(2,128)S(1)}, u32[]{:S(2)}) copy-start(f32[32,2,128]{2,1,0:T(2,128)S(1)} %copy.8) | copy-start | bytes 98308
  95.9 4.9 %collective-permute-start = (f32[16,128]{1,0:T(8,128)S(1)}, f32[16,128]{1,0:T(8,128)S(1)}, u32[]{:S(2)}, u32[]{:S(2)}) collective-permute-start(f32[16,128]{1,0:T(8,128)S(1)} %bitcast.47), channel_id=1, source_target_pairs={{0,4},{4,8},{8,12},{1,5},{5,9},{9,13},{2,6},{6,10},{10,14},{3,7},{... | collective-permute-start | bytes 24584 | tf_op jit(solution)/shard_map/ppermute | solution.py:30
  99.3 4.4 %collective-permute-start.1 = (f32[16,128]{1,0:T(8,128)S(1)}, f32[16,128]{1,0:T(8,128)S(1)}, u32[]{:S(2)}, u32[]{:S(2)}) collective-permute-start(f32[16,128]{1,0:T(8,128)S(1)} %bitcast.46), channel_id=1, source_target_pairs={{4,0},{8,4},{12,8},{5,1},{9,5},{13,9},{6,2},{10,6},{14,10},{7,3},{... | collective-permute-start | bytes 24584 | tf_op jit(solution)/shard_map/ppermute | solution.py:33
  103.8 6.6 %collective-permute-start.2 = (f32[64,16]{1,0:T(8,128)S(1)}, f32[64,16]{1,0:T(8,128)S(1)}, u32[]{:S(2)}, u32[]{:S(2)}) collective-permute-start(f32[64,16]{1,0:T(8,128)S(1)} %get-tuple-element.20), channel_id=1, source_target_pairs={{0,1},{1,2},{2,3},{4,5},{5,6},{6,7},{8,9},{9,10},{10,11},{12,13},{... | collective-permute-start | bytes 12296 | tf_op jit(solution)/shard_map/ppermute | solution.py:30
  108.4 5.2 %collective-permute-start.3 = (f32[64,16]{1,0:T(8,128)S(1)}, f32[64,16]{1,0:T(8,128)S(1)}, u32[]{:S(2)}, u32[]{:S(2)}) collective-permute-start(f32[64,16]{1,0:T(8,128)S(1)} %get-tuple-element.21), channel_id=1, source_target_pairs={{1,0},{2,1},{3,2},{5,4},{6,5},{7,6},{9,8},{10,9},{11,10},{13,12},{... | collective-permute-start | bytes 12296 | tf_op jit(solution)/shard_map/ppermute | solution.py:33
  114.2 4.4 %collective-permute-start.4 = (f32[16,128]{1,0:T(8,128)S(1)}, f32[16,128]{1,0:T(8,128)S(1)}, u32[]{:S(2)}, u32[]{:S(2)}) collective-permute-start(f32[16,128]{1,0:T(8,128)S(1)} %get-tuple-element.22), channel_id=1, source_target_pairs={{0,4},{4,8},{8,12},{1,5},{5,9},{9,13},{2,6},{6,10},{10,14},{3,7},{... | collective-permute-start | bytes 24584 | tf_op jit(solution)/shard_map/ppermute | solution.py:30
  117.4 4.4 %collective-permute-start.5 = (f32[16,128]{1,0:T(8,128)S(1)}, f32[16,128]{1,0:T(8,128)S(1)}, u32[]{:S(2)}, u32[]{:S(2)}) collective-permute-start(f32[16,128]{1,0:T(8,128)S(1)} %get-tuple-element.23), channel_id=1, source_target_pairs={{4,0},{8,4},{12,8},{5,1},{9,5},{13,9},{6,2},{10,6},{14,10},{7,3},{... | collective-permute-start | bytes 24584 | tf_op jit(solution)/shard_map/ppermute | solution.py:33
  121.8 5.3 %collective-permute-start.6 = (f32[64,16]{1,0:T(8,128)S(1)}, f32[64,16]{1,0:T(8,128)S(1)}, u32[]{:S(2)}, u32[]{:S(2)}) collective-permute-start(f32[64,16]{1,0:T(8,128)S(1)} %get-tuple-element.16), channel_id=1, source_target_pairs={{0,1},{1,2},{2,3},{4,5},{5,6},{6,7},{8,9},{9,10},{10,11},{12,13},{... | collective-permute-start | bytes 12296 | tf_op jit(solution)/shard_map/ppermute | solution.py:30
  125.2 5.2 %collective-permute-start.7 = (f32[64,16]{1,0:T(8,128)S(1)}, f32[64,16]{1,0:T(8,128)S(1)}, u32[]{:S(2)}, u32[]{:S(2)}) collective-permute-start(f32[64,16]{1,0:T(8,128)S(1)} %get-tuple-element.17), channel_id=1, source_target_pairs={{1,0},{2,1},{3,2},{5,4},{6,5},{7,6},{9,8},{10,9},{11,10},{13,12},{... | collective-permute-start | bytes 12296 | tf_op jit(solution)/shard_map/ppermute | solution.py:33
Sparse Core Ops, SparseCore 0:
  12.2 54.4 all-reduce.2
  84.4 7.0 reduce-scatter.3
where the time goes:
time: 139 us
  waiting for transfers between devices  67.5 us (49%)
  starting transfers between devices  21 us (15%)
  local copies, waits for them, and re-layouts  16.7 us (12%)
  other arithmetic  16.5 us (12%)
  between operations  15.6 us (11%)
    psum x1, waiting for transfers between devices, from_root(): return lax.psum(block, axis)  47.8 us
    ppermute x4, starting transfers between devices, padded_2(): lax.ppermute(lax.slice_in_dim(block, block.shape[dim] - width, None, axis...  14.5 us
    unnamed x8, local copies, waits for them, and re-layouts  14.2 us
    ppermute x4, waiting for transfers between devices, padded_2(): lax.ppermute(lax.slice_in_dim(block, 0, width, axis=dim), axis, backward)  12.6 us
    unnamed x3, waiting for transfers between devices  7.14 us
    ppermute x4, starting transfers between devices, padded_2(): lax.ppermute(lax.slice_in_dim(block, 0, width, axis=dim), axis, backward)  6.43 us
    convert_element_type x1, other arithmetic, rephase(): (real_part * cosine - imag_part * sine_part).astype(jnp.bfloat16)  6.23 us
    convert_element_type x1, other arithmetic, range_table(): (jnp.cos(phase_angle) * norm_scale).astype(jnp.bfloat16)  4.48 us
  transfers between devices with their start and end apart: 10, of which 6 were waited for; matrix products, arithmetic and copies ran while one was open for 5% of the time, Pallas kernels for 0%

commit v1 on v0

v1 whole, which is shorter than its diff:
```python
import math

import jax
import jax.numpy as jnp
import numpy as np
from jax import lax
from jax.experimental import pallas as pl
from jax.experimental.pallas import tpu as pltpu
from jax.sharding import PartitionSpec as P

F = 1024
PB = 256
NBLK = 2
TR = 32
TC = 128
RAD = 16
LANES = 128
CHUNK = 4

SIGMA_RANGE = 1.0
LOG2E = math.log2(math.e)
OUTSIDE = 1.0e18
MESH = pl.DeviceIdType.MESH


def range_table(chip_cols):
    index = np.arange(F)[:, None] * np.arange(chip_cols)[None, :] % F
    angle = 2.0 * np.pi * index / F
    table = np.concatenate([np.cos(angle), -np.sin(angle)], axis=1) / math.sqrt(F)
    return jnp.asarray(table.astype(np.float32), jnp.bfloat16)


def wrap(index, count):
    if count & (count - 1) == 0:
        return index & (count - 1)
    return lax.rem(lax.rem(index, count) + count, count)


def cos_sin(index, count):
    quarters = index.astype(jnp.float32) * (4.0 / count)
    nearest = jnp.floor(quarters + 0.5)
    x = (quarters - nearest) * (0.5 * math.pi)
    x2 = x * x
    sine = x * (1.0 + x2 * (-1.0 / 6 + x2 * (1.0 / 120 + x2 * (-1.0 / 5040))))
    cosine = 1.0 + x2 * (-0.5 + x2 * (1.0 / 24 + x2 * (-1.0 / 720 + x2 * (1.0 / 40320))))
    turn = nearest.astype(jnp.int32)
    odd = (turn & 1) == 1
    base_c = jnp.where(odd, sine, cosine)
    base_s = jnp.where(odd, cosine, sine)
    c = jnp.where(((turn + 1) & 2) == 2, -base_c, base_c)
    s = jnp.where((turn & 2) == 2, -base_s, base_s)
    return c, s


def smooth(field, left, right):
    center = field[RAD : RAD + TR, :]
    lane = lax.broadcasted_iota(jnp.int32, (TR, TC), 1)
    beside = jnp.where(lane < RAD, right[...], left[...])
    numerator = center
    weight = jnp.ones_like(center)
    for distance in range(1, RAD + 1):
        spatial = 2.0 * distance * distance / (RAD * RAD) * LOG2E
        above = field[RAD - distance : RAD - distance + TR, :]
        below = field[RAD + distance : RAD + distance + TR, :]
        after = pltpu.roll(jnp.where(lane < distance, beside, center), TC - distance, 1)
        before = pltpu.roll(jnp.where(lane >= TC - distance, beside, center), distance, 1)
        for near in (above, below, after, before):
            contrast = near - center
            kernel = jnp.exp2(
                -spatial - contrast * contrast * (0.5 * LOG2E / (SIGMA_RANGE * SIGMA_RANGE))
            )
            numerator = numerator + kernel * near
            weight = weight + kernel
    return numerator / weight


def make_kernel(n_rows, n_cols, n_subs):
    all_rows = TR * n_rows
    chip_cols = n_subs * TC
    n_tiles = n_cols * n_subs
    half = PB // n_subs
    chunk = min(CHUNK, n_rows)
    lines = chunk * TR

    def kernel(
        owner_ref, centres_ref, pulses_hbm, table_hbm, image_ref, despeckled_ref,
        pulses, table, shifts, part, part_in, wire, wire_in, fields, lefts, rights,
        load_sem, shift_send, shift_recv, sub_send, sub_recv, row_send, row_recv,
        halo_send, halo_recv,
    ):
        row = lax.axis_index("row")
        col = lax.axis_index("col")
        sub = lax.axis_index("sub")
        place = col * n_subs + sub
        other = 1 - sub

        load_pulses = pltpu.make_async_copy(pulses_hbm, pulses, load_sem.at[0])
        load_table = pltpu.make_async_copy(table_hbm, table, load_sem.at[1])
        load_pulses.start()
        load_table.start()

        for step in range(2):
            fields[step, 0:RAD, :] = jnp.full((RAD, TC), OUTSIDE, jnp.float32)
            fields[step, RAD + TR :, :] = jnp.full((RAD, TC), OUTSIDE, jnp.float32)
            lefts[step] = jnp.full((TR, TC), OUTSIDE, jnp.float32)
            rights[step] = jnp.full((TR, TC), OUTSIDE, jnp.float32)
        packed = centres_ref[0, 0, 0] * 65536 + centres_ref[0, 0, 1]
        shifts[row] = jnp.full((8, LANES), packed, jnp.int32)

        def beside(step):
            where = place + step
            return {"col": where // n_subs, "sub": where % n_subs}

        has_left = place > 0
        has_right = place < n_tiles - 1
        has_above = row > 0
        has_below = row < n_rows - 1

        barrier = pltpu.get_barrier_semaphore()
        for step in range(1, n_rows):
            pl.semaphore_signal(
                barrier, inc=1, device_id={"row": lax.rem(row + step, n_rows)}, device_id_type=MESH
            )

        @pl.when(has_left)
        def _():
            pl.semaphore_signal(barrier, inc=1, device_id=beside(-1), device_id_type=MESH)

        @pl.when(has_right)
        def _():
            pl.semaphore_signal(barrier, inc=1, device_id=beside(1), device_id_type=MESH)

        pl.semaphore_wait(
            barrier, n_rows - 1 + has_left.astype(jnp.int32) + has_right.astype(jnp.int32)
        )

        shift_copies = []
        for step in range(1, n_rows):
            copy = pltpu.make_async_remote_copy(
                src_ref=shifts.at[row],
                dst_ref=shifts.at[row],
                send_sem=shift_send.at[step],
                recv_sem=shift_recv.at[step],
                device_id={"row": lax.rem(row + step, n_rows)},
                device_id_type=MESH,
            )
            copy.start()
            shift_copies.append(copy)
        for copy in shift_copies:
            copy.wait()

        load_pulses.wait()
        load_table.wait()

        mine = [
            jnp.where(owner_ref[block] == row, 1.0 / math.sqrt(NBLK * PB), 0.0)
            for block in range(NBLK)
        ]

        def form(first):
            real_lines, imag_lines = [], []
            lane = lax.broadcasted_iota(jnp.int32, (TR, half), 1)
            line = lax.broadcasted_iota(jnp.int32, (TR, half), 0)
            packs = [shifts[first + tile] for tile in range(chunk)]
            for tile in range(chunk):
                down = jnp.concatenate([packs[tile][:, :1] >> 16] * (TR // 8), axis=0)
                lines_at = (first + tile) * TR + line - down
                real_line, imag_line = [], []
                for block in range(NBLK):
                    pulse = block * PB + sub * half + lane
                    c, s = cos_sin(wrap(pulse * lines_at, all_rows), all_rows)
                    c = (c * mine[block]).astype(jnp.bfloat16)
                    s = (s * mine[block]).astype(jnp.bfloat16)
                    real_line += [c, s]
                    imag_line += [-s, c]
                real_lines.append(jnp.concatenate(real_line, axis=1))
                imag_lines.append(jnp.concatenate(imag_line, axis=1))
            azimuth = jnp.concatenate(real_lines + imag_lines, axis=0)
            focused = jnp.dot(azimuth, pulses[...], preferred_element_type=jnp.float32)
            turned_real, turned_imag = [], []
            for tile in range(chunk):
                across = packs[tile][:, :1] & 65535
                frequency = lax.broadcasted_iota(jnp.int32, (8, F), 1)
                c, s = cos_sin(wrap(frequency * (across - col * chip_cols), F), F)
                c = jnp.concatenate([c] * (TR // 8), axis=0)
                s = jnp.concatenate([s] * (TR // 8), axis=0)
                real = focused[tile * TR : (tile + 1) * TR]
                imag = focused[lines + tile * TR : lines + (tile + 1) * TR]
                turned_real.append((real * c - imag * s).astype(jnp.bfloat16))
                turned_imag.append((real * s + imag * c).astype(jnp.bfloat16))
            turned = jnp.concatenate(turned_real + turned_imag, axis=0)
            product = jnp.dot(turned, table[...], preferred_element_type=jnp.float32)
            real = product[:lines, :chip_cols] - product[lines:, chip_cols:]
            imag = product[:lines, chip_cols:] + product[lines:, :chip_cols]
            for which in range(n_subs):
                for tile in range(chunk):
                    at = slice(tile * TR, (tile + 1) * TR)
                    cut = slice(which * TC, (which + 1) * TC)
                    part[which, first + tile, 0] = real[at, cut]
                    part[which, first + tile, 1] = imag[at, cut]

        if chunk == n_rows:
            form(0)
        else:

            def body(index, carry):
                form(index * chunk)
                return carry

            lax.fori_loop(0, n_rows // chunk, body, 0)

        to_other = pltpu.make_async_remote_copy(
            src_ref=part.at[other],
            dst_ref=part_in,
            send_sem=sub_send,
            recv_sem=sub_recv,
            device_id={"sub": other},
            device_id_type=MESH,
        )
        to_other.start()
        to_other.wait()

        row_copies = []
        for step in range(1, n_rows):
            target = lax.rem(row + step, n_rows)
            wire[step] = (part[sub, target] + part_in[target]).astype(jnp.bfloat16)
            copy = pltpu.make_async_remote_copy(
                src_ref=wire.at[step],
                dst_ref=wire_in.at[step],
                send_sem=row_send.at[step],
                recv_sem=row_recv.at[step],
                device_id={"row": target},
                device_id_type=MESH,
            )
            copy.start()
            row_copies.append(copy)
        image = part[sub, row] + part_in[row]
        for copy in row_copies:
            copy.wait()
        for step in range(1, n_rows):
            image = image + wire_in[step].astype(jnp.float32)
        image_ref[:, 0, :] = image[0]
        image_ref[:, 1, :] = image[1]
        field = image[0] * image[0] + image[1] * image[1]

        for step in range(2):
            fields[step, RAD : RAD + TR, :] = field
            low = fields.at[step, RAD : 2 * RAD]
            high = fields.at[step, TR : RAD + TR]
            whole = fields.at[step, RAD : RAD + TR]
            plans = (
                (has_above, has_below, low, fields.at[step, RAD + TR :], {"row": row - 1}),
                (has_below, has_above, high, fields.at[step, 0:RAD], {"row": row + 1}),
                (has_left, has_right, whole, rights.at[step], beside(-1)),
                (has_right, has_left, whole, lefts.at[step], beside(1)),
            )
            copies = []
            for number, (sends, receives, source, target, device) in enumerate(plans):
                copy = pltpu.make_async_remote_copy(
                    src_ref=source,
                    dst_ref=target,
                    send_sem=halo_send.at[step, number],
                    recv_sem=halo_recv.at[step, number],
                    device_id=device,
                    device_id_type=MESH,
                )
                copies.append((sends, receives, copy))

                @pl.when(sends)
                def _():
                    copy.start()

            for sends, receives, copy in copies:

                @pl.when(receives)
                def _():
                    copy.wait_recv()

            field = smooth(fields.at[step], lefts.at[step], rights.at[step])
            for sends, receives, copy in copies:

                @pl.when(sends)
                def _():
                    copy.wait_send()

        despeckled_ref[...] = field

    dma = pltpu.SemaphoreType.DMA
    vmem = pl.BlockSpec(memory_space=pltpu.VMEM)
    smem = pl.BlockSpec(memory_space=pltpu.SMEM)
    hbm = pl.BlockSpec(memory_space=pl.ANY)
    depth = NBLK * 2 * half
    return pl.pallas_call(
        kernel,
        out_shape=(
            jax.ShapeDtypeStruct((TR, 2, TC), jnp.float32),
            jax.ShapeDtypeStruct((TR, TC), jnp.float32),
        ),
        in_specs=[smem, smem, hbm, hbm],
        out_specs=(vmem, vmem),
        scratch_shapes=[
            pltpu.VMEM((depth, F), jnp.bfloat16),
            pltpu.VMEM((F, 2 * chip_cols), jnp.bfloat16),
            pltpu.VMEM((n_rows, 8, LANES), jnp.int32),
            pltpu.VMEM((n_subs, n_rows, 2, TR, TC), jnp.float32),
            pltpu.VMEM((n_rows, 2, TR, TC), jnp.float32),
            pltpu.VMEM((n_rows, 2, TR, TC), jnp.bfloat16),
            pltpu.VMEM((n_rows, 2, TR, TC), jnp.bfloat16),
            pltpu.VMEM((2, TR + 2 * RAD, TC), jnp.float32),
            pltpu.VMEM((2, TR, TC), jnp.float32),
            pltpu.VMEM((2, TR, TC), jnp.float32),
            dma((2,)),
            dma((n_rows,)),
            dma((n_rows,)),
            dma,
            dma,
            dma((n_rows,)),
            dma((n_rows,)),
            dma((2, 4)),
            dma((2, 4)),
        ],
        compiler_params=pltpu.CompilerParams(
            collective_id=0, has_side_effects=True, vmem_limit_bytes=40 * 2**20
        ),
        cost_estimate=pl.CostEstimate(
            flops=4 * lines * depth * F * 2, bytes_accessed=3 * 2**20, transcendentals=2**20
        ),
    )


def solution(mesh):
    n_rows, n_cols, n_subs = (mesh.shape[name] for name in ("row", "col", "sub"))
    call = make_kernel(n_rows, n_cols, n_subs)
    table = range_table(n_subs * TC)

    def per_device(pulses, owner, centres):
        return call(owner, centres, pulses.reshape(-1, F), table)

    return jax.shard_map(
        per_device,
        mesh=mesh,
        in_specs=(
            P(None, ("groups", "row"), None, "sub", None),
            P("groups"),
            P(("groups", "row"), "col", None),
        ),
        out_specs=(
            P(("groups", "row"), None, ("col", "sub")),
            P(("groups", "row"), ("col", "sub")),
        ),
        check_vma=False,
    )
```

time: 139 us -> 26.9 us (0.19)
  the two profiles are of different devices: /device:TPU:1 before, /device:TPU:0 now
where the time goes in v1:
time: 26.9 us; the launch traced here: 26.7 us
  Pallas kernels  21.8 us (81%)
  local copies, waits for them, and re-layouts  4.33 us (16%)
  between operations  0.66 us (2%)
    pallas_call x1, Pallas kernels, per_device(): return call(owner, centres, pulses.reshape(-1, F), table)  21.8 us
    unnamed x10, local copies, waits for them, and re-layouts  4.33 us

profile of v1, /device:TPU:0, one launch (start us, length us, event | category | flops | bytes accessed | tf_op | source)
XLA Modules:
  0.0 26.7 jit_solution(13024959331575524522)
XLA Ops:
  0.6 0.0 copy-start.3
  0.6 0.0 copy-start.2
  0.6 0.6 %copy-done.3 = s32[1,1,2]{2,1,0:T(1,128)S(1)} copy-done((s32[1,1,2]{2,1,0:T(1,128)S(1)}, s32[1,1,2]{2,1,0:T(1,128)}, u32[]{:S(2)}) %copy-start.3) | copy-done | bytes 32
  1.3 0.0 copy-done.2
  1.3 0.0 copy-start
  1.3 1.2 %copy-done = bf16[2,1,2,128,1024]{4,3,2,1,0:T(8,128)(2,1)S(1)} copy-done((bf16[2,1,2,128,1024]{4,3,2,1,0:T(8,128)(2,1)S(1)}, bf16[2,1,2,128,1024]{4,3,2,1,0:T(8,128)(2,1)}, u32[]{:S(2)}) %copy-start) | copy-done | bytes 1048600
  2.5 0.0 copy-start.1
  2.5 1.2 %copy-done.1 = bf16[1024,512]{1,0:T(8,128)(2,1)S(1)} copy-done((bf16[1024,512]{1,0:T(8,128)(2,1)S(1)}, bf16[1024,512]{1,0:T(8,128)(2,1)}, u32[]{:S(2)}) %copy-start.1) | copy-done | bytes 1048600
  3.8 21.8 %shard_map.59 = (f32[32,2,128]{2,1,0:T(2,128)S(1)}, f32[32,128]{1,0:T(8,128)S(1)}) custom-call(s32[2]{0:T(128)S(1)} %copy-done.2, s32[1,1,2]{2,1,0:T(1,128)S(1)} %copy-done.3, bf16[512,1024]{1,0:T(8,128)(2,1)S(1)} %bitcast.1, bf16[1024,512]{1,0:T(8,128)(2,1)S(1)} %copy-done.1), custom_call_target="tpu_custom_call" | custom-call | flops 536870912 | bytes 3145728 | tf_op jit(solution)/shard_map/pallas_call | solution.py:337
  25.5 0.6 %copy.8 = f32[32,2,128]{2,1,0:T(2,128)} copy(f32[32,2,128]{2,1,0:T(2,128)S(1)} %get-tuple-element.4) | data formatting | bytes 65536
  26.1 0.6 %copy.9 = f32[32,128]{1,0:T(8,128)} copy(f32[32,128]{1,0:T(8,128)S(1)} %get-tuple-element.5) | data formatting | bytes 32768
Async XLA Ops:
  0.6 0.7 %copy-start.3 = (s32[1,1,2]{2,1,0:T(1,128)S(1)}, s32[1,1,2]{2,1,0:T(1,128)}, u32[]{:S(2)}) copy-start(s32[1,1,2]{2,1,0:T(1,128)} %centres_ref.1) | copy-start | bytes 28
  0.6 0.7 %copy-start.2 = (s32[2]{0:T(128)S(1)}, s32[2]{0:T(128)}, u32[]{:S(2)}) copy-start(s32[2]{0:T(128)} %owner_ref.1) | copy-start | bytes 28
  1.3 1.2 %copy-start = (bf16[2,1,2,128,1024]{4,3,2,1,0:T(8,128)(2,1)S(1)}, bf16[2,1,2,128,1024]{4,3,2,1,0:T(8,128)(2,1)}, u32[]{:S(2)}) copy-start(bf16[2,1,2,128,1024]{4,3,2,1,0:T(8,128)(2,1)} %param.4) | copy-start | bytes 3145732
  2.5 1.2 %copy-start.1 = (bf16[1024,512]{1,0:T(8,128)(2,1)S(1)}, bf16[1024,512]{1,0:T(8,128)(2,1)}, u32[]{:S(2)}) copy-start(bf16[1024,512]{1,0:T(8,128)(2,1)} %constant.2.clone.table_hbm) | copy-start | bytes 3145732

commit v2 on v1

--- a/solution.py
+++ b/solution.py
@@ -20,20 +20,28 @@
 SIGMA_RANGE = 1.0
 LOG2E = math.log2(math.e)
 OUTSIDE = 1.0e18
+UNIT = math.sqrt(0.5 * LOG2E) / SIGMA_RANGE
 MESH = pl.DeviceIdType.MESH
 
 
-def range_table(chip_cols):
-    index = np.arange(F)[:, None] * np.arange(chip_cols)[None, :] % F
-    angle = 2.0 * np.pi * index / F
-    table = np.concatenate([np.cos(angle), -np.sin(angle)], axis=1) / math.sqrt(F)
+def constant(table):
     return jnp.asarray(table.astype(np.float32), jnp.bfloat16)
 
 
-def wrap(index, count):
-    if count & (count - 1) == 0:
-        return index & (count - 1)
-    return lax.rem(lax.rem(index, count) + count, count)
+def range_table(n_subs):
+    index = np.arange(F)[:, None] * np.arange(n_subs * TC)[None, :] % F
+    angle = (2.0 * np.pi / F * index).reshape(F, n_subs, TC).transpose(1, 0, 2)
+    return constant(np.concatenate([np.cos(angle), -np.sin(angle)], axis=2) / math.sqrt(F))
+
+
+def azimuth_table(all_rows, n_subs):
+    index = np.arange(all_rows)[:, None] * np.arange(NBLK * PB)[None, :] % all_rows
+    angle = (2.0 * np.pi / all_rows * index).reshape(all_rows, NBLK, n_subs, PB // n_subs)
+    c = np.cos(angle).transpose(2, 0, 1, 3)
+    s = np.sin(angle).transpose(2, 0, 1, 3)
+    parts = [np.stack([c, s], axis=3), np.stack([-s, c], axis=3)]
+    table = np.concatenate([part.reshape(n_subs, all_rows, -1) for part in parts], axis=1)
+    return constant(table / math.sqrt(NBLK * PB))
 
 
 def cos_sin(index, count):
@@ -66,9 +74,7 @@
         before = pltpu.roll(jnp.where(lane >= TC - distance, beside, center), distance, 1)
         for near in (above, below, after, before):
             contrast = near - center
-            kernel = jnp.exp2(
-                -spatial - contrast * contrast * (0.5 * LOG2E / (SIGMA_RANGE * SIGMA_RANGE))
-            )
+            kernel = jnp.exp2(-spatial - contrast * contrast)
             numerator = numerator + kernel * near
             weight = weight + kernel
     return numerator / weight
@@ -79,12 +85,13 @@
     chip_cols = n_subs * TC
     n_tiles = n_cols * n_subs
     half = PB // n_subs
+    depth = NBLK * 2 * half
     chunk = min(CHUNK, n_rows)
     lines = chunk * TR
 
     def kernel(
-        owner_ref, centres_ref, pulses_hbm, table_hbm, image_ref, despeckled_ref,
-        pulses, table, shifts, part, part_in, wire, wire_in, fields, lefts, rights,
+        owner_hbm, centres_hbm, pulses_hbm, azimuth_hbm, table_hbm, image_ref, despeckled_ref,
+        owner, centres, pulses, azimuth, table, focused_real, focused_imag, shifts, part, part_in, wire, wire_in, fields, lefts, rights,
         load_sem, shift_send, shift_recv, sub_send, sub_recv, row_send, row_recv,
         halo_send, halo_recv,
     ):
@@ -94,19 +101,27 @@
         place = col * n_subs + sub
         other = 1 - sub
 
-        load_pulses = pltpu.make_async_copy(pulses_hbm, pulses, load_sem.at[0])
-        load_table = pltpu.make_async_copy(table_hbm, table, load_sem.at[1])
-        load_pulses.start()
-        load_table.start()
+        loads = [
+            pltpu.make_async_copy(source, target, load_sem.at[number])
+            for number, (source, target) in enumerate(
+                (
+                    (centres_hbm, centres),
+                    (owner_hbm, owner),
+                    (azimuth_hbm.at[sub], azimuth),
+                    (pulses_hbm, pulses),
+                    (table_hbm, table),
+                )
+            )
+        ]
+        load_centres, load_owner, load_azimuth, load_pulses, load_table = loads
+        for load in loads:
+            load.start()
 
         for step in range(2):
             fields[step, 0:RAD, :] = jnp.full((RAD, TC), OUTSIDE, jnp.float32)
             fields[step, RAD + TR :, :] = jnp.full((RAD, TC), OUTSIDE, jnp.float32)
             lefts[step] = jnp.full((TR, TC), OUTSIDE, jnp.float32)
             rights[step] = jnp.full((TR, TC), OUTSIDE, jnp.float32)
-        packed = centres_ref[0, 0, 0] * 65536 + centres_ref[0, 0, 1]
-        shifts[row] = jnp.full((8, LANES), packed, jnp.int32)
-
         def beside(step):
             where = place + step
             return {"col": where // n_subs, "sub": where % n_subs}
@@ -129,6 +144,10 @@
         @pl.when(has_right)
         def _():
             pl.semaphore_signal(barrier, inc=1, device_id=beside(1), device_id_type=MESH)
+
+        load_centres.wait()
+        packed = centres[0, 0, 0] * 65536 + centres[0, 0, 1]
+        shifts[row] = jnp.full((8, LANES), packed, jnp.int32)
 
         pl.semaphore_wait(
             barrier, n_rows - 1 + has_left.astype(jnp.int32) + has_right.astype(jnp.int32)
@@ -146,68 +165,55 @@
             )
             copy.start()
             shift_copies.append(copy)
+
+        load_owner.wait()
+        load_azimuth.wait()
+        which_block = lax.broadcasted_iota(jnp.int32, (1, depth), 1) // (2 * half)
+        mine = jnp.zeros((1, depth), jnp.float32)
+        for block in range(NBLK):
+            held = jnp.where(owner[block] == row, 1.0, 0.0)
+            mine = jnp.where(which_block == block, held, mine)
+        masked = azimuth[...] * mine.astype(jnp.bfloat16)
+        load_pulses.wait()
+        focused = jnp.dot(masked, pulses[...], preferred_element_type=jnp.float32)
+        for target, values in (
+            (focused_real, focused[:all_rows]), (focused_imag, focused[all_rows:])
+        ):
+            for group in range(F // LANES):
+                cut = values[:, group * LANES : (group + 1) * LANES]
+                target[group, TR:, :] = cut
+                target[group, 0:TR, :] = cut[all_rows - TR :]
+
         for copy in shift_copies:
             copy.wait()
-
-        load_pulses.wait()
         load_table.wait()
 
-        mine = [
-            jnp.where(owner_ref[block] == row, 1.0 / math.sqrt(NBLK * PB), 0.0)
-            for block in range(NBLK)
-        ]
-
-        def form(first):
-            real_lines, imag_lines = [], []
-            lane = lax.broadcasted_iota(jnp.int32, (TR, half), 1)
-            line = lax.broadcasted_iota(jnp.int32, (TR, half), 0)
-            packs = [shifts[first + tile] for tile in range(chunk)]
-            for tile in range(chunk):
-                down = jnp.concatenate([packs[tile][:, :1] >> 16] * (TR // 8), axis=0)
-                lines_at = (first + tile) * TR + line - down
-                real_line, imag_line = [], []
-                for block in range(NBLK):
-                    pulse = block * PB + sub * half + lane
-                    c, s = cos_sin(wrap(pulse * lines_at, all_rows), all_rows)
-                    c = (c * mine[block]).astype(jnp.bfloat16)
-                    s = (s * mine[block]).astype(jnp.bfloat16)
-                    real_line += [c, s]
-                    imag_line += [-s, c]
-                real_lines.append(jnp.concatenate(real_line, axis=1))
-                imag_lines.append(jnp.concatenate(imag_line, axis=1))
-            azimuth = jnp.concatenate(real_lines + imag_lines, axis=0)
-            focused = jnp.dot(azimuth, pulses[...], preferred_element_type=jnp.float32)
+        def turn(first):
             turned_real, turned_imag = [], []
             for tile in range(chunk):
-                across = packs[tile][:, :1] & 65535
+                pack = shifts[first + tile]
+                down = pack[0, 0] >> 16
+                across = (pack[:, :1] & 65535) - col * chip_cols
                 frequency = lax.broadcasted_iota(jnp.int32, (8, F), 1)
-                c, s = cos_sin(wrap(frequency * (across - col * chip_cols), F), F)
+                c, s = cos_sin((frequency * across) & (F - 1), F)
                 c = jnp.concatenate([c] * (TR // 8), axis=0)
                 s = jnp.concatenate([s] * (TR // 8), axis=0)
-                real = focused[tile * TR : (tile + 1) * TR]
-                imag = focused[lines + tile * TR : lines + (tile + 1) * TR]
+                at = pl.ds((first + tile + 1) * TR - down, TR)
+                groups = range(F // LANES)
+                real = jnp.concatenate([focused_real[group, at, :] for group in groups], axis=1)
+                imag = jnp.concatenate([focused_imag[group, at, :] for group in groups], axis=1)
                 turned_real.append((real * c - imag * s).astype(jnp.bfloat16))
                 turned_imag.append((real * s + imag * c).astype(jnp.bfloat16))
-            turned = jnp.concatenate(turned_real + turned_imag, axis=0)
-            product = jnp.dot(turned, table[...], preferred_element_type=jnp.float32)
-            real = product[:lines, :chip_cols] - product[lines:, chip_cols:]
-            imag = product[:lines, chip_cols:] + product[lines:, :chip_cols]
-            for which in range(n_subs):
-                for tile in range(chunk):
-                    at = slice(tile * TR, (tile + 1) * TR)
-                    cut = slice(which * TC, (which + 1) * TC)
-                    part[which, first + tile, 0] = real[at, cut]
-                    part[which, first + tile, 1] = imag[at, cut]
-
-        if chunk == n_rows:
-            form(0)
-        else:
-
-            def body(index, carry):
-                form(index * chunk)
-                return carry
-
-            lax.fori_loop(0, n_rows // chunk, body, 0)
+            return jnp.concatenate(turned_real + turned_imag, axis=0)
+
+        def form(turned, first, which):
+            product = jnp.dot(turned, table[which], preferred_element_type=jnp.float32)
+            real = product[:lines, :TC] - product[lines:, TC:]
+            imag = product[:lines, TC:] + product[lines:, :TC]
+            for tile in range(chunk):
+                at = slice(tile * TR, (tile + 1) * TR)
+                part[which, first + tile, 0] = real[at]
+                part[which, first + tile, 1] = imag[at]
 
         to_other = pltpu.make_async_remote_copy(
             src_ref=part.at[other],
@@ -217,7 +223,21 @@
             device_id={"sub": other},
             device_id_type=MESH,
         )
-        to_other.start()
+        if chunk == n_rows:
+            turned = turn(0)
+            form(turned, 0, other)
+            to_other.start()
+            form(turned, 0, sub)
+        else:
+
+            def body(index, carry):
+                turned = turn(index * chunk)
+                form(turned, index * chunk, other)
+                form(turned, index * chunk, sub)
+                return carry
+
+            lax.fori_loop(0, n_rows // chunk, body, 0)
+            to_other.start()
         to_other.wait()
 
         row_copies = []
@@ -241,7 +261,7 @@
             image = image + wire_in[step].astype(jnp.float32)
         image_ref[:, 0, :] = image[0]
         image_ref[:, 1, :] = image[1]
-        field = image[0] * image[0] + image[1] * image[1]
+        field = (image[0] * image[0] + image[1] * image[1]) * UNIT
 
         for step in range(2):
             fields[step, RAD : RAD + TR, :] = field
@@ -283,24 +303,27 @@
                 def _():
                     copy.wait_send()
 
-        despeckled_ref[...] = field
+        despeckled_ref[...] = field * (1.0 / UNIT)
 
     dma = pltpu.SemaphoreType.DMA
     vmem = pl.BlockSpec(memory_space=pltpu.VMEM)
-    smem = pl.BlockSpec(memory_space=pltpu.SMEM)
-    hbm = pl.BlockSpec(memory_space=pl.ANY)
-    depth = NBLK * 2 * half
+    hbm = pl.BlockSpec(memory_space=pltpu.HBM)
     return pl.pallas_call(
         kernel,
         out_shape=(
             jax.ShapeDtypeStruct((TR, 2, TC), jnp.float32),
             jax.ShapeDtypeStruct((TR, TC), jnp.float32),
         ),
-        in_specs=[smem, smem, hbm, hbm],
+        in_specs=[hbm] * 5,
         out_specs=(vmem, vmem),
         scratch_shapes=[
+            pltpu.SMEM((NBLK,), jnp.int32),
+            pltpu.SMEM((1, 1, 2), jnp.int32),
             pltpu.VMEM((depth, F), jnp.bfloat16),
-            pltpu.VMEM((F, 2 * chip_cols), jnp.bfloat16),
+            pltpu.VMEM((2 * all_rows, depth), jnp.bfloat16),
+            pltpu.VMEM((n_subs, F, 2 * TC), jnp.bfloat16),
+            pltpu.VMEM((F // LANES, TR + all_rows, LANES), jnp.float32),
+            pltpu.VMEM((F // LANES, TR + all_rows, LANES), jnp.float32),
             pltpu.VMEM((n_rows, 8, LANES), jnp.int32),
             pltpu.VMEM((n_subs, n_rows, 2, TR, TC), jnp.float32),
             pltpu.VMEM((n_rows, 2, TR, TC), jnp.float32),
@@ -309,7 +332,7 @@
             pltpu.VMEM((2, TR + 2 * RAD, TC), jnp.float32),
             pltpu.VMEM((2, TR, TC), jnp.float32),
             pltpu.VMEM((2, TR, TC), jnp.float32),
-            dma((2,)),
+            dma((5,)),
             dma((n_rows,)),
             dma((n_rows,)),
             dma,
@@ -320,7 +343,7 @@
             dma((2, 4)),
         ],
         compiler_params=pltpu.CompilerParams(
-            collective_id=0, has_side_effects=True, vmem_limit_bytes=40 * 2**20
+            collective_id=0, has_side_effects=True, vmem_limit_bytes=60 * 2**20
         ),
         cost_estimate=pl.CostEstimate(
             flops=4 * lines * depth * F * 2, bytes_accessed=3 * 2**20, transcendentals=2**20
@@ -331,10 +354,11 @@
 def solution(mesh):
     n_rows, n_cols, n_subs = (mesh.shape[name] for name in ("row", "col", "sub"))
     call = make_kernel(n_rows, n_cols, n_subs)
-    table = range_table(n_subs * TC)
+    azimuth = azimuth_table(TR * n_rows, n_subs)
+    table = range_table(n_subs)
 
     def per_device(pulses, owner, centres):
-        return call(owner, centres, pulses.reshape(-1, F), table)
+        return call(owner, centres, pulses.reshape(-1, F), azimuth, table)
 
     return jax.shard_map(
         per_device,

time: 26.9 us -> 23.8 us (0.88)
  local copies, waits for them, and re-layouts: 4.33 us -> 1.99 us
  Pallas kernels: 21.8 us -> 21 us
    unnamed x10 -> x4, local copies, waits for them, and re-layouts: 4.33 us -> 1.99 us
    pallas_call x1, Pallas kernels: 21.8 us -> 21 us  [per_device(): return call(owner, centres, pulses.reshape(-1, F), azimuth, table)]
where the time goes in v2:
time: 23.8 us; the launch traced here: 23.6 us
  Pallas kernels  21 us (88%)
  local copies, waits for them, and re-layouts  1.99 us (8%)
  between operations  0.65 us (3%)
    pallas_call x1, Pallas kernels, per_device(): return call(owner, centres, pulses.reshape(-1, F), azimuth, table)  21 us
    unnamed x4, local copies, waits for them, and re-layouts  1.99 us

profile of v2, /device:TPU:0, one launch (start us, length us, event | category | flops | bytes accessed | tf_op | source)
XLA Modules:
  0.0 23.6 jit_solution(10803630093196733016)
XLA Ops:
  0.6 21.0 %shard_map.68 = (f32[32,2,128]{2,1,0:T(2,128)}, f32[32,128]{1,0:T(8,128)}) custom-call(s32[2]{0:T(128)} %owner_hbm.1, s32[1,1,2]{2,1,0:T(1,128)} %centres_hbm.1, bf16[512,1024]{1,0:T(8,128)(2,1)} %bitcast.1, bf16[2,256,512]{2,1,0:T(8,128)(2,1)} %constant.4.clone.azimuth_hbm, bf16[2,1024,256]{2,1,0:T(8,128)(2,1)} %constant.5.clone.table_hbm), custom_call_target="tpu_custom_call" | custom-call | flops 536870912 | bytes 3145728 | tf_op jit(solution)/shard_map/pallas_call | solution.py:361
  21.6 0.0 copy-start
  21.6 1.4 %copy.9 = f32[32,2,128]{2,1,0:T(2,128)} copy(f32[32,2,128]{2,1,0:T(2,128)} %get-tuple-element.4) | data formatting | bytes 65536
  23.0 0.0 copy-done
  23.0 0.6 %copy.10 = f32[32,128]{1,0:T(8,128)} copy(f32[32,128]{1,0:T(8,128)S(1)} %copy-done) | data formatting | bytes 32768
Async XLA Ops:
  21.6 1.4 %copy-start = (f32[32,128]{1,0:T(8,128)S(1)}, f32[32,128]{1,0:T(8,128)}, u32[]{:S(2)}) copy-start(f32[32,128]{1,0:T(8,128)} %get-tuple-element.5) | copy-start | bytes 49156

commit v3 on v2

--- a/solution.py
+++ b/solution.py
@@ -60,24 +60,66 @@
     return c, s
 
 
-def smooth(field, left, right):
-    center = field[RAD : RAD + TR, :]
-    lane = lax.broadcasted_iota(jnp.int32, (TR, TC), 1)
-    beside = jnp.where(lane < RAD, right[...], left[...])
-    numerator = center
-    weight = jnp.ones_like(center)
-    for distance in range(1, RAD + 1):
-        spatial = 2.0 * distance * distance / (RAD * RAD) * LOG2E
-        above = field[RAD - distance : RAD - distance + TR, :]
-        below = field[RAD + distance : RAD + distance + TR, :]
-        after = pltpu.roll(jnp.where(lane < distance, beside, center), TC - distance, 1)
-        before = pltpu.roll(jnp.where(lane >= TC - distance, beside, center), distance, 1)
-        for near in (above, below, after, before):
-            contrast = near - center
-            kernel = jnp.exp2(-spatial - contrast * contrast)
-            numerator = numerator + kernel * near
-            weight = weight + kernel
-    return numerator / weight
+def add(sums, near, center, spatial):
+    contrast = near - center
+    kernel = jnp.exp2(-spatial - contrast * contrast)
+    return sums[0] + kernel * near, sums[1] + kernel
+
+
+SPATIAL = [2.0 * d * d / (RAD * RAD) * LOG2E for d in range(RAD + 1)]
+
+
+def begin(field):
+    centers = [field[RAD + first : RAD + first + 8, :] for first in range(0, TR, 8)]
+    return [(center, jnp.ones_like(center)) for center in centers]
+
+
+def along_rows(field, sums, inner):
+    result = []
+    for number, first in enumerate(range(0, TR, 8)):
+        center = field[RAD + first : RAD + first + 8, :]
+        total = sums[number]
+        for distance in range(1, RAD + 1):
+            for low in (first - distance, first + distance):
+                if (0 <= low <= TR - 8) == inner:
+                    near = field[RAD + low : RAD + low + 8, :]
+                    total = add(total, near, center, SPATIAL[distance])
+        result.append(total)
+    return result
+
+
+def along_cols(field, outer, sums):
+    result = []
+    lane = lax.broadcasted_iota(jnp.int32, (8, TC), 1)
+    for number, first in enumerate(range(0, TR, 8)):
+        center = field[RAD + first : RAD + first + 8, :]
+        outside = outer[first : first + 8, :]
+        total = sums[number]
+        for distance in range(1, RAD + 1):
+            after = pltpu.roll(jnp.where(lane < distance, outside, center), TC - distance, 1)
+            before = pltpu.roll(jnp.where(lane >= TC - distance, outside, center), distance, 1)
+            for near in (after, before):
+                total = add(total, near, center, SPATIAL[distance])
+        result.append(total)
+    return result
+
+
+def ratio(sums):
+    return jnp.concatenate([numerator / weight for numerator, weight in sums], axis=0)
+
+
+def last_pass(packed, image_hbm, despeckled_ref, image, image_sem):
+    image[:, 0, :] = packed[0:TR, :]
+    image[:, 1, :] = packed[TR : 2 * TR, :]
+    copy = pltpu.make_async_copy(image, image_hbm, image_sem)
+    copy.start()
+    field = packed.at[2 * TR : 4 * TR]
+    outer = packed[4 * TR : 5 * TR, :]
+    sums = along_rows(field, begin(field), True)
+    sums = along_rows(field, sums, False)
+    sums = along_cols(field, outer, sums)
+    despeckled_ref[...] = ratio(sums) * (1.0 / UNIT)
+    copy.wait()
 
 
 def make_kernel(n_rows, n_cols, n_subs):
@@ -90,8 +132,8 @@
     lines = chunk * TR
 
     def kernel(
-        owner_hbm, centres_hbm, pulses_hbm, azimuth_hbm, table_hbm, image_ref, despeckled_ref,
-        owner, centres, pulses, azimuth, table, focused_real, focused_imag, shifts, part, part_in, wire, wire_in, fields, lefts, rights,
+        owner_hbm, centres_hbm, pulses_hbm, azimuth_hbm, table_hbm, packed_ref,
+        owner, centres, pulses, pulses_in, azimuth, table, focused_real, focused_imag, shifts, part, wire, wire_in, fields, lefts, rights,
         load_sem, shift_send, shift_recv, sub_send, sub_recv, row_send, row_recv,
         halo_send, halo_recv,
     ):
@@ -107,9 +149,9 @@
                 (
                     (centres_hbm, centres),
                     (owner_hbm, owner),
-                    (azimuth_hbm.at[sub], azimuth),
+                    (azimuth_hbm, azimuth),
                     (pulses_hbm, pulses),
-                    (table_hbm, table),
+                    (table_hbm.at[sub], table),
                 )
             )
         ]
@@ -166,6 +208,16 @@
             copy.start()
             shift_copies.append(copy)
 
+        to_other = pltpu.make_async_remote_copy(
+            src_ref=pulses_hbm,
+            dst_ref=pulses_in,
+            send_sem=sub_send,
+            recv_sem=sub_recv,
+            device_id={"sub": other},
+            device_id_type=MESH,
+        )
+        to_other.start()
+
         load_owner.wait()
         load_azimuth.wait()
         which_block = lax.broadcasted_iota(jnp.int32, (1, depth), 1) // (2 * half)
@@ -173,20 +225,24 @@
         for block in range(NBLK):
             held = jnp.where(owner[block] == row, 1.0, 0.0)
             mine = jnp.where(which_block == block, held, mine)
-        masked = azimuth[...] * mine.astype(jnp.bfloat16)
+        mine = mine.astype(jnp.bfloat16)
         load_pulses.wait()
-        focused = jnp.dot(masked, pulses[...], preferred_element_type=jnp.float32)
-        for target, values in (
-            (focused_real, focused[:all_rows]), (focused_imag, focused[all_rows:])
-        ):
+        focused = jnp.dot(azimuth[sub] * mine, pulses[...], preferred_element_type=jnp.float32)
+        halves = ((focused_real, slice(0, all_rows)), (focused_imag, slice(all_rows, None)))
+        for target, at in halves:
             for group in range(F // LANES):
-                cut = values[:, group * LANES : (group + 1) * LANES]
-                target[group, TR:, :] = cut
-                target[group, 0:TR, :] = cut[all_rows - TR :]
-
+                target[group, TR:, :] = focused[at, group * LANES : (group + 1) * LANES]
+        to_other.wait_recv()
+        focused = jnp.dot(azimuth[other] * mine, pulses_in[...], preferred_element_type=jnp.float32)
+        for target, at in halves:
+            for group in range(F // LANES):
+                total = target[group, TR:, :] + focused[at, group * LANES : (group + 1) * LANES]
+                target[group, TR:, :] = total
+                target[group, 0:TR, :] = total[all_rows - TR :]
+
+        load_table.wait()
         for copy in shift_copies:
-            copy.wait()
-        load_table.wait()
+            copy.wait_recv()
 
         def turn(first):
             turned_real, turned_imag = [], []
@@ -206,46 +262,32 @@
                 turned_imag.append((real * s + imag * c).astype(jnp.bfloat16))
             return jnp.concatenate(turned_real + turned_imag, axis=0)
 
-        def form(turned, first, which):
-            product = jnp.dot(turned, table[which], preferred_element_type=jnp.float32)
+        def form(first):
+            product = jnp.dot(turn(first), table[...], preferred_element_type=jnp.float32)
             real = product[:lines, :TC] - product[lines:, TC:]
             imag = product[:lines, TC:] + product[lines:, :TC]
             for tile in range(chunk):
                 at = slice(tile * TR, (tile + 1) * TR)
-                part[which, first + tile, 0] = real[at]
-                part[which, first + tile, 1] = imag[at]
-
-        to_other = pltpu.make_async_remote_copy(
-            src_ref=part.at[other],
-            dst_ref=part_in,
-            send_sem=sub_send,
-            recv_sem=sub_recv,
-            device_id={"sub": other},
-            device_id_type=MESH,
-        )
+                part[first + tile, 0] = real[at]
+                part[first + tile, 1] = imag[at]
+                wire[first + tile, 0] = real[at].astype(jnp.bfloat16)
+                wire[first + tile, 1] = imag[at].astype(jnp.bfloat16)
+
         if chunk == n_rows:
-            turned = turn(0)
-            form(turned, 0, other)
-            to_other.start()
-            form(turned, 0, sub)
+            form(0)
         else:
 
             def body(index, carry):
-                turned = turn(index * chunk)
-                form(turned, index * chunk, other)
-                form(turned, index * chunk, sub)
+                form(index * chunk)
                 return carry
 
             lax.fori_loop(0, n_rows // chunk, body, 0)
-            to_other.start()
-        to_other.wait()
 
         row_copies = []
         for step in range(1, n_rows):
             target = lax.rem(row + step, n_rows)
-            wire[step] = (part[sub, target] + part_in[target]).astype(jnp.bfloat16)
             copy = pltpu.make_async_remote_copy(
-                src_ref=wire.at[step],
+                src_ref=wire.at[target],
                 dst_ref=wire_in.at[step],
                 send_sem=row_send.at[step],
                 recv_sem=row_recv.at[step],
@@ -254,27 +296,26 @@
             )
             copy.start()
             row_copies.append(copy)
-        image = part[sub, row] + part_in[row]
-        for copy in row_copies:
-            copy.wait()
-        for step in range(1, n_rows):
+        image = part[row]
+        for step, copy in enumerate(row_copies, 1):
+            copy.wait_recv()
             image = image + wire_in[step].astype(jnp.float32)
-        image_ref[:, 0, :] = image[0]
-        image_ref[:, 1, :] = image[1]
         field = (image[0] * image[0] + image[1] * image[1]) * UNIT
 
-        for step in range(2):
+        sent = []
+
+        def exchange(step, field):
             fields[step, RAD : RAD + TR, :] = field
             low = fields.at[step, RAD : 2 * RAD]
             high = fields.at[step, TR : RAD + TR]
             whole = fields.at[step, RAD : RAD + TR]
             plans = (
+                (has_left, has_right, whole, rights.at[step], beside(-1)),
+                (has_right, has_left, whole, lefts.at[step], beside(1)),
                 (has_above, has_below, low, fields.at[step, RAD + TR :], {"row": row - 1}),
                 (has_below, has_above, high, fields.at[step, 0:RAD], {"row": row + 1}),
-                (has_left, has_right, whole, rights.at[step], beside(-1)),
-                (has_right, has_left, whole, lefts.at[step], beside(1)),
             )
-            copies = []
+            arriving = []
             for number, (sends, receives, source, target, device) in enumerate(plans):
                 copy = pltpu.make_async_remote_copy(
                     src_ref=source,
@@ -284,48 +325,64 @@
                     device_id=device,
                     device_id_type=MESH,
                 )
-                copies.append((sends, receives, copy))
+                sent.append((sends, copy))
+                arriving.append((receives, copy))
 
                 @pl.when(sends)
                 def _():
                     copy.start()
 
-            for sends, receives, copy in copies:
+            return arriving
+
+        def arrive(arriving):
+            for receives, copy in arriving:
 
                 @pl.when(receives)
                 def _():
                     copy.wait_recv()
 
-            field = smooth(fields.at[step], lefts.at[step], rights.at[step])
-            for sends, receives, copy in copies:
-
-                @pl.when(sends)
-                def _():
-                    copy.wait_send()
-
-        despeckled_ref[...] = field * (1.0 / UNIT)
+        line = lax.broadcasted_iota(jnp.int32, (TR, TC), 1)
+        arriving = exchange(0, field)
+        packed_ref[0:TR, :] = image[0]
+        packed_ref[TR : 2 * TR, :] = image[1]
+        first = fields.at[0]
+        sums = along_rows(first, begin(first), True)
+        arrive(arriving)
+        sums = along_rows(first, sums, False)
+        outer = jnp.where(line < RAD, rights[0], lefts[0])
+        field = ratio(along_cols(first, outer, sums))
+
+        arriving = exchange(1, field)
+        to_other.wait_send()
+        for copy in shift_copies + row_copies:
+            copy.wait_send()
+        arrive(arriving)
+        packed_ref[2 * TR : 4 * TR, :] = fields[1]
+        packed_ref[4 * TR :, :] = jnp.where(line < RAD, rights[1], lefts[1])
+        for sends, copy in sent:
+
+            @pl.when(sends)
+            def _():
+                copy.wait_send()
 
     dma = pltpu.SemaphoreType.DMA
     vmem = pl.BlockSpec(memory_space=pltpu.VMEM)
     hbm = pl.BlockSpec(memory_space=pltpu.HBM)
-    return pl.pallas_call(
+    form_call = pl.pallas_call(
         kernel,
-        out_shape=(
-            jax.ShapeDtypeStruct((TR, 2, TC), jnp.float32),
-            jax.ShapeDtypeStruct((TR, TC), jnp.float32),
-        ),
+        out_shape=jax.ShapeDtypeStruct((5 * TR, TC), jnp.float32),
         in_specs=[hbm] * 5,
-        out_specs=(vmem, vmem),
+        out_specs=vmem,
         scratch_shapes=[
             pltpu.SMEM((NBLK,), jnp.int32),
             pltpu.SMEM((1, 1, 2), jnp.int32),
             pltpu.VMEM((depth, F), jnp.bfloat16),
-            pltpu.VMEM((2 * all_rows, depth), jnp.bfloat16),
-            pltpu.VMEM((n_subs, F, 2 * TC), jnp.bfloat16),
+            pltpu.VMEM((depth, F), jnp.bfloat16),
+            pltpu.VMEM((n_subs, 2 * all_rows, depth), jnp.bfloat16),
+            pltpu.VMEM((F, 2 * TC), jnp.bfloat16),
             pltpu.VMEM((F // LANES, TR + all_rows, LANES), jnp.float32),
             pltpu.VMEM((F // LANES, TR + all_rows, LANES), jnp.float32),
             pltpu.VMEM((n_rows, 8, LANES), jnp.int32),
-            pltpu.VMEM((n_subs, n_rows, 2, TR, TC), jnp.float32),
             pltpu.VMEM((n_rows, 2, TR, TC), jnp.float32),
             pltpu.VMEM((n_rows, 2, TR, TC), jnp.bfloat16),
             pltpu.VMEM((n_rows, 2, TR, TC), jnp.bfloat16),
@@ -343,22 +400,34 @@
             dma((2, 4)),
         ],
         compiler_params=pltpu.CompilerParams(
-            collective_id=0, has_side_effects=True, vmem_limit_bytes=60 * 2**20
+            collective_id=0, has_side_effects=True, vmem_limit_bytes=int(53.5 * 2**20)
         ),
         cost_estimate=pl.CostEstimate(
             flops=4 * lines * depth * F * 2, bytes_accessed=3 * 2**20, transcendentals=2**20
         ),
     )
+    last_call = pl.pallas_call(
+        last_pass,
+        out_shape=(
+            jax.ShapeDtypeStruct((TR, 2, TC), jnp.float32),
+            jax.ShapeDtypeStruct((TR, TC), jnp.float32),
+        ),
+        in_specs=[vmem],
+        out_specs=(hbm, vmem),
+        scratch_shapes=[pltpu.VMEM((TR, 2, TC), jnp.float32), dma],
+        cost_estimate=pl.CostEstimate(flops=2**20, bytes_accessed=2**17, transcendentals=2**18),
+    )
+    return form_call, last_call
 
 
 def solution(mesh):
     n_rows, n_cols, n_subs = (mesh.shape[name] for name in ("row", "col", "sub"))
-    call = make_kernel(n_rows, n_cols, n_subs)
+    form_call, last_call = make_kernel(n_rows, n_cols, n_subs)
     azimuth = azimuth_table(TR * n_rows, n_subs)
     table = range_table(n_subs)
 
     def per_device(pulses, owner, centres):
-        return call(owner, centres, pulses.reshape(-1, F), azimuth, table)
+        return last_call(form_call(owner, centres, pulses.reshape(-1, F), azimuth, table))
 
     return jax.shard_map(
         per_device,

time: 23.8 us -> 23.3 us (0.979)
  local copies, waits for them, and re-layouts: 1.99 us -> 1.27 us
    unnamed x4 -> x6, local copies, waits for them, and re-layouts: 1.99 us -> 1.27 us
    pallas_call x1 -> x2, Pallas kernels: 21 us -> 21.2 us  [the longest x1 18.8 us: per_device(): form_call(owner, centres, pulses.reshape(-1, F), azimuth, table)]
where the time goes in v3:
time: 23.3 us; the launch traced here: 23.2 us
  Pallas kernels  21.2 us (91%)
  local copies, waits for them, and re-layouts  1.27 us (5%)
  between operations  0.66 us (3%)
    pallas_call x1, Pallas kernels, per_device(): form_call(owner, centres, pulses.reshape(-1, F), azimuth, table)  18.8 us
    pallas_call x1, Pallas kernels, per_device(): last_call(form_call(owner, centres, pulses.reshape(-1, F), azimuth, table))  2.39 us
    unnamed x6, local copies, waits for them, and re-layouts  1.27 us

profile of v3, /device:TPU:0, one launch (start us, length us, event | category | flops | bytes accessed | tf_op | source)
XLA Modules:
  0.0 23.2 jit_solution(8484770702026266321)
XLA Ops:
  0.6 0.0 copy-start.2
  0.6 0.0 copy-start.1
  0.7 0.6 %copy-done.2 = s32[1,1,2]{2,1,0:T(1,128)S(1)} copy-done((s32[1,1,2]{2,1,0:T(1,128)S(1)}, s32[1,1,2]{2,1,0:T(1,128)}, u32[]{:S(2)}) %copy-start.2) | copy-done | bytes 32
  1.3 0.0 copy-done.1
  1.3 18.8 %shard_map.68.packed = f32[160,128]{1,0:T(8,128)S(1)} custom-call(s32[2]{0:T(128)S(1)} %copy-done.1, s32[1,1,2]{2,1,0:T(1,128)S(1)} %copy-done.2, bf16[512,1024]{1,0:T(8,128)(2,1)} %bitcast.1, bf16[2,256,512]{2,1,0:T(8,128)(2,1)} %constant.4.clone.azimuth_hbm, bf16[2,1024,256]{2,1,0:T(8,128)(2,1)} %constant.5.clone.table_hbm), custom_call_target="tpu_custom_call" | custom-call | flops 536870912 | bytes 3145728 | tf_op jit(solution)/shard_map/pallas_call | solution.py:430
  20.1 0.0 copy-start
  20.2 0.6 %copy-done = f32[160,128]{1,0:T(8,128)} copy-done((f32[160,128]{1,0:T(8,128)}, f32[160,128]{1,0:T(8,128)S(1)}, u32[]{:S(2)}) %copy-start) | copy-done | bytes 81944
  20.8 2.4 %shard_map.69 = (f32[32,2,128]{2,1,0:T(2,128)}, f32[32,128]{1,0:T(8,128)}) custom-call(f32[160,128]{1,0:T(8,128)} %copy-done), custom_call_target="tpu_custom_call" | custom-call | flops 1048576 | bytes 131072 | tf_op jit(solution)/shard_map/pallas_call | solution.py:430
Async XLA Ops:
  0.6 0.7 %copy-start.2 = (s32[1,1,2]{2,1,0:T(1,128)S(1)}, s32[1,1,2]{2,1,0:T(1,128)}, u32[]{:S(2)}) copy-start(s32[1,1,2]{2,1,0:T(1,128)} %centres_hbm.1) | copy-start | bytes 28
  0.6 0.7 %copy-start.1 = (s32[2]{0:T(128)S(1)}, s32[2]{0:T(128)}, u32[]{:S(2)}) copy-start(s32[2]{0:T(128)} %owner_hbm.1) | copy-start | bytes 28
  20.1 0.6 %copy-start = (f32[160,128]{1,0:T(8,128)}, f32[160,128]{1,0:T(8,128)S(1)}, u32[]{:S(2)}) copy-start(f32[160,128]{1,0:T(8,128)S(1)} %shard_map.68.packed) | copy-start | bytes 245764

commit v4 on v3

v4 whole, which is shorter than its diff:
```python
import math

import jax
import jax.numpy as jnp
import numpy as np
from jax import lax
from jax.experimental import pallas as pl
from jax.experimental.pallas import tpu as pltpu
from jax.sharding import PartitionSpec as P

F = 1024
PB = 256
NBLK = 2
TR = 32
TC = 128
RAD = 16
LANES = 128

SIGMA_RANGE = 1.0
LOG2E = math.log2(math.e)
OUTSIDE = 1.0e18
UNIT = math.sqrt(0.5 * LOG2E) / SIGMA_RANGE
MESH = pl.DeviceIdType.MESH


def constant(table):
    return jnp.asarray(table.astype(np.float32), jnp.bfloat16)


def range_table():
    index = np.arange(F)[:, None] * np.arange(F)[None, :] % F
    angle = (2.0 * np.pi / F * index).reshape(F, F // TC, TC).transpose(1, 0, 2)
    return constant(np.concatenate([np.cos(angle), -np.sin(angle)], axis=2) / math.sqrt(F))


def azimuth_table(all_rows, n_subs):
    index = np.arange(all_rows)[:, None] * np.arange(NBLK * PB)[None, :] % all_rows
    angle = (2.0 * np.pi / all_rows * index).reshape(all_rows, NBLK, n_subs, PB // n_subs)
    c = np.cos(angle).transpose(2, 0, 1, 3)
    s = np.sin(angle).transpose(2, 0, 1, 3)
    parts = [np.stack([c, s], axis=3), np.stack([-s, c], axis=3)]
    table = np.concatenate([part.reshape(n_subs, all_rows, -1) for part in parts], axis=1)
    return constant(table / math.sqrt(NBLK * PB))


def add(sums, nears, center, distance):
    top = bottom = None
    for near in nears:
        contrast = near - center
        kernel = jnp.exp2(-SPATIAL[distance] - contrast * contrast)
        term = kernel * near
        top = term if top is None else top + term
        bottom = kernel if bottom is None else bottom + kernel
    return (sums[0] + top, sums[1] + bottom) if nears else sums


SPATIAL = [2.0 * d * d / (RAD * RAD) * LOG2E for d in range(RAD + 1)]


def begin(field):
    centers = [field[RAD + first : RAD + first + 8, :] for first in range(0, TR, 8)]
    return [(center, jnp.ones_like(center)) for center in centers]


def along_rows(field, sums, inner):
    sums = list(sums)
    centers = [field[RAD + first : RAD + first + 8, :] for first in range(0, TR, 8)]
    for distance in range(1, RAD + 1):
        for number, first in enumerate(range(0, TR, 8)):
            nears = [
                field[RAD + low : RAD + low + 8, :]
                for low in (first - distance, first + distance)
                if (0 <= low <= TR - 8) == inner
            ]
            sums[number] = add(sums[number], nears, centers[number], distance)
    return sums


def along_cols(field, outer, sums):
    sums = list(sums)
    lane = lax.broadcasted_iota(jnp.int32, (8, TC), 1)
    centers = [field[RAD + first : RAD + first + 8, :] for first in range(0, TR, 8)]
    outers = [outer[first : first + 8, :] for first in range(0, TR, 8)]
    for distance in range(1, RAD + 1):
        for number, (center, outside) in enumerate(zip(centers, outers)):
            after = jnp.where(lane < distance, outside, center)
            before = jnp.where(lane >= TC - distance, outside, center)
            nears = [
                pltpu.roll(after, TC - distance, 1),
                pltpu.roll(before, distance, 1),
            ]
            sums[number] = add(sums[number], nears, center, distance)
    return sums


def ratio(sums):
    return jnp.concatenate([numerator / weight for numerator, weight in sums], axis=0)


def last_pass(packed, image_hbm, despeckled_hbm, image, despeckled, sems):
    image[:, 0, :] = packed[0:TR, :]
    image[:, 1, :] = packed[TR : 2 * TR, :]
    save_image = pltpu.make_async_copy(image, image_hbm, sems.at[0])
    save_image.start()
    field = packed.at[2 * TR : 4 * TR]
    outer = packed[4 * TR : 5 * TR, :]
    sums = along_rows(field, begin(field), True)
    sums = along_rows(field, sums, False)
    sums = along_cols(field, outer, sums)
    despeckled[...] = ratio(sums) * (1.0 / UNIT)
    save = pltpu.make_async_copy(despeckled, despeckled_hbm, sems.at[1])
    save.start()
    save_image.wait()
    save.wait()


def make_kernel(n_rows, n_cols, n_subs):
    all_rows = TR * n_rows
    n_tiles = n_cols * n_subs
    half = PB // n_subs
    depth = NBLK * 2 * half

    def kernel(
        owner_hbm, centres_hbm, pulses_hbm, azimuth_hbm, table_hbm, packed_ref,
        owner, centres, pulses, azimuth, table, focus, focus_out, focus_in, formed, shifts, wire, wire_in, fields, lefts, rights,
        load_sem, shift_send, shift_recv, sub_send, sub_recv, row_send, row_recv,
        halo_send, halo_recv,
    ):
        row = lax.axis_index("row")
        col = lax.axis_index("col")
        sub = lax.axis_index("sub")
        place = col * n_subs + sub
        other = 1 - sub

        loads = [
            pltpu.make_async_copy(source, target, load_sem.at[number])
            for number, (source, target) in enumerate(
                (
                    (centres_hbm, centres),
                    (owner_hbm, owner),
                    (azimuth_hbm.at[sub], azimuth),
                    (pulses_hbm, pulses),
                    (table_hbm.at[lax.rem(place + F // TC - 1, F // TC)], table.at[0]),
                    (table_hbm.at[lax.rem(place, F // TC)], table.at[1]),
                )
            )
        ]
        load_centres, load_owner, load_azimuth, load_pulses, *load_tables = loads
        for load in loads:
            load.start()

        for step in range(2):
            fields[step, 0:RAD, :] = jnp.full((RAD, TC), OUTSIDE, jnp.float32)
            fields[step, RAD + TR :, :] = jnp.full((RAD, TC), OUTSIDE, jnp.float32)
            lefts[step] = jnp.full((TR, TC), OUTSIDE, jnp.float32)
            rights[step] = jnp.full((TR, TC), OUTSIDE, jnp.float32)
        def beside(step):
            where = place + step
            return {"col": where // n_subs, "sub": where % n_subs}

        has_left = place > 0
        has_right = place < n_tiles - 1
        has_above = row > 0
        has_below = row < n_rows - 1

        barrier = pltpu.get_barrier_semaphore()
        for step in range(1, n_rows):
            pl.semaphore_signal(
                barrier, inc=1, device_id={"row": lax.rem(row + step, n_rows)}, device_id_type=MESH
            )

        @pl.when(has_left)
        def _():
            pl.semaphore_signal(barrier, inc=1, device_id=beside(-1), device_id_type=MESH)

        @pl.when(has_right)
        def _():
            pl.semaphore_signal(barrier, inc=1, device_id=beside(1), device_id_type=MESH)

        load_centres.wait()
        packed = centres[0, 0, 0] * 65536 + centres[0, 0, 1]
        shifts[row] = jnp.full((8, LANES), packed, jnp.int32)

        load_owner.wait()
        load_azimuth.wait()
        which_block = lax.broadcasted_iota(jnp.int32, (1, depth), 1) // (2 * half)
        mine = jnp.zeros((1, depth), jnp.float32)
        for block in range(NBLK):
            held = jnp.where(owner[block] == row, 1.0, 0.0)
            mine = jnp.where(which_block == block, held, mine)
        masked = azimuth[...] * mine.astype(jnp.bfloat16)

        pl.semaphore_wait(
            barrier, n_rows - 1 + has_left.astype(jnp.int32) + has_right.astype(jnp.int32)
        )

        shift_copies = []
        for step in range(1, n_rows):
            copy = pltpu.make_async_remote_copy(
                src_ref=shifts.at[row],
                dst_ref=shifts.at[row],
                send_sem=shift_send.at[step],
                recv_sem=shift_recv.at[step],
                device_id={"row": lax.rem(row + step, n_rows)},
                device_id_type=MESH,
            )
            copy.start()
            shift_copies.append(copy)

        load_pulses.wait()
        focused = jnp.dot(masked, pulses[...], preferred_element_type=jnp.float32)
        focus_out[...] = focused.astype(jnp.bfloat16)
        to_other = pltpu.make_async_remote_copy(
            src_ref=focus_out,
            dst_ref=focus_in,
            send_sem=sub_send,
            recv_sem=sub_recv,
            device_id={"sub": other},
            device_id_type=MESH,
        )
        to_other.start()
        focus[...] = focused
        for load in load_tables:
            load.wait()
        to_other.wait_recv()
        whole = (focus[...] + focus_in[...].astype(jnp.float32)).astype(jnp.bfloat16)
        for side in range(2):
            product = jnp.dot(whole, table[side], preferred_element_type=jnp.float32)
            real = product[:all_rows, :TC] - product[all_rows:, TC:]
            imag = product[:all_rows, TC:] + product[all_rows:, :TC]
            for number, values in enumerate((real, imag)):
                formed[number, side, TR:, :] = values
                formed[number, side, 0:TR, :] = values[all_rows - TR :]

        for copy in shift_copies:
            copy.wait_recv()
        line = lax.broadcasted_iota(jnp.int32, (TR, TC), 1)

        def tile_of(which):
            packed = shifts[which][0, 0]
            down = packed >> 16
            across = packed & 65535
            at = pl.ds((which + 1) * TR - down, TR)
            parts = []
            for number in range(2):
                values = jnp.where(
                    line < TC - across, formed[number, 1, at, :], formed[number, 0, at, :]
                )
                parts.append(pltpu.roll(values, across, 1))
            return parts

        row_copies = []
        for step in range(1, n_rows):
            target = lax.rem(row + step, n_rows)
            for number, values in enumerate(tile_of(target)):
                wire[step, number] = values.astype(jnp.bfloat16)
            copy = pltpu.make_async_remote_copy(
                src_ref=wire.at[step],
                dst_ref=wire_in.at[step],
                send_sem=row_send.at[step],
                recv_sem=row_recv.at[step],
                device_id={"row": target},
                device_id_type=MESH,
            )
            copy.start()
            row_copies.append(copy)
        image = tile_of(row)
        for step, copy in enumerate(row_copies, 1):
            copy.wait_recv()
            image = [image[number] + wire_in[step, number].astype(jnp.float32) for number in range(2)]
        field = (image[0] * image[0] + image[1] * image[1]) * UNIT

        sent = []

        def exchange(step, field):
            fields[step, RAD : RAD + TR, :] = field
            low = fields.at[step, RAD : 2 * RAD]
            high = fields.at[step, TR : RAD + TR]
            whole = fields.at[step, RAD : RAD + TR]
            plans = (
                (has_left, has_right, whole, rights.at[step], beside(-1)),
                (has_right, has_left, whole, lefts.at[step], beside(1)),
                (has_above, has_below, low, fields.at[step, RAD + TR :], {"row": row - 1}),
                (has_below, has_above, high, fields.at[step, 0:RAD], {"row": row + 1}),
            )
            arriving = []
            for number, (sends, receives, source, target, device) in enumerate(plans):
                copy = pltpu.make_async_remote_copy(
                    src_ref=source,
                    dst_ref=target,
                    send_sem=halo_send.at[step, number],
                    recv_sem=halo_recv.at[step, number],
                    device_id=device,
                    device_id_type=MESH,
                )
                sent.append((sends, copy))
                arriving.append((receives, copy))

                @pl.when(sends)
                def _():
                    copy.start()

            return arriving

        def arrive(arriving):
            for receives, copy in arriving:

                @pl.when(receives)
                def _():
                    copy.wait_recv()

        arriving = exchange(0, field)
        packed_ref[0:TR, :] = image[0]
        packed_ref[TR : 2 * TR, :] = image[1]
        first = fields.at[0]
        sums = along_rows(first, begin(first), True)
        arrive(arriving)
        sums = along_rows(first, sums, False)
        outer = jnp.where(line < RAD, rights[0], lefts[0])
        field = ratio(along_cols(first, outer, sums))

        arriving = exchange(1, field)
        to_other.wait_send()
        for copy in shift_copies + row_copies:
            copy.wait_send()
        arrive(arriving)
        packed_ref[2 * TR : 4 * TR, :] = fields[1]
        packed_ref[4 * TR :, :] = jnp.where(line < RAD, rights[1], lefts[1])
        for sends, copy in sent:

            @pl.when(sends)
            def _():
                copy.wait_send()

    dma = pltpu.SemaphoreType.DMA
    vmem = pl.BlockSpec(memory_space=pltpu.VMEM)
    hbm = pl.BlockSpec(memory_space=pltpu.HBM)
    form_call = pl.pallas_call(
        kernel,
        out_shape=jax.ShapeDtypeStruct((5 * TR, TC), jnp.float32),
        in_specs=[hbm] * 5,
        out_specs=vmem,
        scratch_shapes=[
            pltpu.SMEM((NBLK,), jnp.int32),
            pltpu.SMEM((1, 1, 2), jnp.int32),
            pltpu.VMEM((depth, F), jnp.bfloat16),
            pltpu.VMEM((2 * all_rows, depth), jnp.bfloat16),
            pltpu.VMEM((2, F, 2 * TC), jnp.bfloat16),
            pltpu.VMEM((2 * all_rows, F), jnp.float32),
            pltpu.VMEM((2 * all_rows, F), jnp.bfloat16),
            pltpu.VMEM((2 * all_rows, F), jnp.bfloat16),
            pltpu.VMEM((2, 2, TR + all_rows, TC), jnp.float32),
            pltpu.VMEM((n_rows, 8, LANES), jnp.int32),
            pltpu.VMEM((n_rows, 2, TR, TC), jnp.bfloat16),
            pltpu.VMEM((n_rows, 2, TR, TC), jnp.bfloat16),
            pltpu.VMEM((2, TR + 2 * RAD, TC), jnp.float32),
            pltpu.VMEM((2, TR, TC), jnp.float32),
            pltpu.VMEM((2, TR, TC), jnp.float32),
            dma((6,)),
            dma((n_rows,)),
            dma((n_rows,)),
            dma,
            dma,
            dma((n_rows,)),
            dma((n_rows,)),
            dma((2, 4)),
            dma((2, 4)),
        ],
        compiler_params=pltpu.CompilerParams(
            collective_id=0, has_side_effects=True, vmem_limit_bytes=int(53.5 * 2**20)
        ),
        cost_estimate=pl.CostEstimate(
            flops=8 * all_rows * depth * F, bytes_accessed=3 * 2**20, transcendentals=2**20
        ),
    )
    last_call = pl.pallas_call(
        last_pass,
        out_shape=(
            jax.ShapeDtypeStruct((TR, 2, TC), jnp.float32),
            jax.ShapeDtypeStruct((TR, TC), jnp.float32),
        ),
        in_specs=[vmem],
        out_specs=(hbm, hbm),
        scratch_shapes=[
            pltpu.VMEM((TR, 2, TC), jnp.float32),
            pltpu.VMEM((TR, TC), jnp.float32),
            dma((2,)),
        ],
        cost_estimate=pl.CostEstimate(flops=2**20, bytes_accessed=2**17, transcendentals=2**18),
    )
    return form_call, last_call


def solution(mesh):
    n_rows, n_cols, n_subs = (mesh.shape[name] for name in ("row", "col", "sub"))
    form_call, last_call = make_kernel(n_rows, n_cols, n_subs)
    azimuth = azimuth_table(TR * n_rows, n_subs)
    table = range_table()

    def per_device(pulses, owner, centres):
        return last_call(form_call(owner, centres, pulses.reshape(-1, F), azimuth, table))

    return jax.shard_map(
        per_device,
        mesh=mesh,
        in_specs=(
            P(None, ("groups", "row"), None, "sub", None),
            P("groups"),
            P(("groups", "row"), "col", None),
        ),
        out_specs=(
            P(("groups", "row"), None, ("col", "sub")),
            P(("groups", "row"), ("col", "sub")),
        ),
        check_vma=False,
    )
```

time: 23.3 us -> 22.9 us (0.983)
  Pallas kernels: 21.2 us -> 20.1 us
  local copies, waits for them, and re-layouts: 1.27 us -> 1.92 us
    unnamed x6, local copies, waits for them, and re-layouts: 1.27 us -> 1.92 us
    pallas_call x1, Pallas kernels: 2.39 us -> 1.79 us  [per_device(): last_call(form_call(owner, centres, pulses.reshape(-1, F), azimuth, table))]
    pallas_call x1, Pallas kernels: 18.8 us -> 18.3 us  [per_device(): form_call(owner, centres, pulses.reshape(-1, F), azimuth, table)]
where the time goes in v4:
time: 22.9 us; the launch traced here: 22.7 us
  Pallas kernels  20.1 us (88%)
  local copies, waits for them, and re-layouts  1.92 us (8%)
  between operations  0.66 us (3%)
    pallas_call x1, Pallas kernels, per_device(): form_call(owner, centres, pulses.reshape(-1, F), azimuth, table)  18.3 us
    unnamed x6, local copies, waits for them, and re-layouts  1.92 us
    pallas_call x1, Pallas kernels, per_device(): last_call(form_call(owner, centres, pulses.reshape(-1, F), azimuth, table))  1.79 us

profile of v4, /device:TPU:0, one launch (start us, length us, event | category | flops | bytes accessed | tf_op | source)
XLA Modules:
  0.0 22.7 jit_solution(8581664907566392356)
XLA Ops:
  0.6 0.0 copy-start.1
  0.6 0.6 %copy-done.1 = s32[2]{0:T(128)S(1)} copy-done((s32[2]{0:T(128)S(1)}, s32[2]{0:T(128)}, u32[]{:S(2)}) %copy-start.1) | copy-done | bytes 32
  1.3 0.0 copy-start.2
  1.3 0.7 %copy-done.2 = s32[1,1,2]{2,1,0:T(1,128)S(1)} copy-done((s32[1,1,2]{2,1,0:T(1,128)S(1)}, s32[1,1,2]{2,1,0:T(1,128)}, u32[]{:S(2)}) %copy-start.2) | copy-done | bytes 32
  1.9 18.3 %shard_map.68.packed = f32[160,128]{1,0:T(8,128)S(1)} custom-call(s32[2]{0:T(128)S(1)} %copy-done.1, s32[1,1,2]{2,1,0:T(1,128)S(1)} %copy-done.2, bf16[512,1024]{1,0:T(8,128)(2,1)} %bitcast.1, bf16[2,256,512]{2,1,0:T(8,128)(2,1)} %constant.4.clone.azimuth_hbm, bf16[8,1024,256]{2,1,0:T(8,128)(2,1)} %constant.5.clone.table_hbm), custom_call_target="tpu_custom_call" | custom-call | flops 536870912 | bytes 3145728 | tf_op jit(solution)/shard_map/pallas_call | solution.py:401
  20.3 0.0 copy-start
  20.3 0.6 %copy-done = f32[160,128]{1,0:T(8,128)} copy-done((f32[160,128]{1,0:T(8,128)}, f32[160,128]{1,0:T(8,128)S(1)}, u32[]{:S(2)}) %copy-start) | copy-done | bytes 81944
  20.9 1.8 %shard_map.69 = (f32[32,2,128]{2,1,0:T(2,128)}, f32[32,128]{1,0:T(8,128)}) custom-call(f32[160,128]{1,0:T(8,128)} %copy-done), custom_call_target="tpu_custom_call" | custom-call | flops 1048576 | bytes 131072 | tf_op jit(solution)/shard_map/pallas_call | solution.py:401
Async XLA Ops:
  0.6 0.7 %copy-start.1 = (s32[2]{0:T(128)S(1)}, s32[2]{0:T(128)}, u32[]{:S(2)}) copy-start(s32[2]{0:T(128)} %owner_hbm.1) | copy-start | bytes 28
  1.3 0.7 %copy-start.2 = (s32[1,1,2]{2,1,0:T(1,128)S(1)}, s32[1,1,2]{2,1,0:T(1,128)}, u32[]{:S(2)}) copy-start(s32[1,1,2]{2,1,0:T(1,128)} %centres_hbm.1) | copy-start | bytes 28
  20.3 0.6 %copy-start = (f32[160,128]{1,0:T(8,128)}, f32[160,128]{1,0:T(8,128)S(1)}, u32[]{:S(2)}) copy-start(f32[160,128]{1,0:T(8,128)S(1)} %shard_map.68.packed) | copy-start | bytes 245764

commit v5 on v4

--- a/solution.py
+++ b/solution.py
@@ -122,7 +122,7 @@
 
     def kernel(
         owner_hbm, centres_hbm, pulses_hbm, azimuth_hbm, table_hbm, packed_ref,
-        owner, centres, pulses, azimuth, table, focus, focus_out, focus_in, formed, shifts, wire, wire_in, fields, lefts, rights,
+        owner, centres, pulses, azimuth, table, formed, shifts, part, part_in, wire, wire_in, fields, lefts, rights,
         load_sem, shift_send, shift_recv, sub_send, sub_recv, row_send, row_recv,
         halo_send, halo_recv,
     ):
@@ -140,8 +140,10 @@
                     (owner_hbm, owner),
                     (azimuth_hbm.at[sub], azimuth),
                     (pulses_hbm, pulses),
-                    (table_hbm.at[lax.rem(place + F // TC - 1, F // TC)], table.at[0]),
-                    (table_hbm.at[lax.rem(place, F // TC)], table.at[1]),
+                    *(
+                        (table_hbm.at[lax.rem(col * n_subs + side + F // TC - 1, F // TC)], table.at[side])
+                        for side in range(n_subs + 1)
+                    ),
                 )
             )
         ]
@@ -208,23 +210,9 @@
             shift_copies.append(copy)
 
         load_pulses.wait()
-        focused = jnp.dot(masked, pulses[...], preferred_element_type=jnp.float32)
-        focus_out[...] = focused.astype(jnp.bfloat16)
-        to_other = pltpu.make_async_remote_copy(
-            src_ref=focus_out,
-            dst_ref=focus_in,
-            send_sem=sub_send,
-            recv_sem=sub_recv,
-            device_id={"sub": other},
-            device_id_type=MESH,
-        )
-        to_other.start()
-        focus[...] = focused
-        for load in load_tables:
+        whole = jnp.dot(masked, pulses[...], preferred_element_type=jnp.float32).astype(jnp.bfloat16)
+        for side, load in enumerate(load_tables):
             load.wait()
-        to_other.wait_recv()
-        whole = (focus[...] + focus_in[...].astype(jnp.float32)).astype(jnp.bfloat16)
-        for side in range(2):
             product = jnp.dot(whole, table[side], preferred_element_type=jnp.float32)
             real = product[:all_rows, :TC] - product[all_rows:, TC:]
             imag = product[:all_rows, TC:] + product[all_rows:, :TC]
@@ -236,7 +224,7 @@
             copy.wait_recv()
         line = lax.broadcasted_iota(jnp.int32, (TR, TC), 1)
 
-        def tile_of(which):
+        def tile_of(which, core):
             packed = shifts[which][0, 0]
             down = packed >> 16
             across = packed & 65535
@@ -244,27 +232,42 @@
             parts = []
             for number in range(2):
                 values = jnp.where(
-                    line < TC - across, formed[number, 1, at, :], formed[number, 0, at, :]
+                    line < TC - across, formed[number, core + 1, at, :], formed[number, core, at, :]
                 )
                 parts.append(pltpu.roll(values, across, 1))
             return parts
 
+        for step in range(n_rows):
+            which = lax.rem(row + step, n_rows)
+            for number, values in enumerate(tile_of(which, other)):
+                part[step, number] = values
+        to_other = pltpu.make_async_remote_copy(
+            src_ref=part,
+            dst_ref=part_in,
+            send_sem=sub_send,
+            recv_sem=sub_recv,
+            device_id={"sub": other},
+            device_id_type=MESH,
+        )
+        to_other.start()
+        tiles = [tile_of(lax.rem(row + step, n_rows), sub) for step in range(n_rows)]
+        to_other.wait_recv()
+
         row_copies = []
         for step in range(1, n_rows):
-            target = lax.rem(row + step, n_rows)
-            for number, values in enumerate(tile_of(target)):
-                wire[step, number] = values.astype(jnp.bfloat16)
+            for number in range(2):
+                wire[step, number] = (tiles[step][number] + part_in[step, number]).astype(jnp.bfloat16)
             copy = pltpu.make_async_remote_copy(
                 src_ref=wire.at[step],
                 dst_ref=wire_in.at[step],
                 send_sem=row_send.at[step],
                 recv_sem=row_recv.at[step],
-                device_id={"row": target},
+                device_id={"row": lax.rem(row + step, n_rows)},
                 device_id_type=MESH,
             )
             copy.start()
             row_copies.append(copy)
-        image = tile_of(row)
+        image = [tiles[0][number] + part_in[0, number] for number in range(2)]
         for step, copy in enumerate(row_copies, 1):
             copy.wait_recv()
             image = [image[number] + wire_in[step, number].astype(jnp.float32) for number in range(2)]
@@ -345,18 +348,17 @@
             pltpu.SMEM((1, 1, 2), jnp.int32),
             pltpu.VMEM((depth, F), jnp.bfloat16),
             pltpu.VMEM((2 * all_rows, depth), jnp.bfloat16),
-            pltpu.VMEM((2, F, 2 * TC), jnp.bfloat16),
-            pltpu.VMEM((2 * all_rows, F), jnp.float32),
-            pltpu.VMEM((2 * all_rows, F), jnp.bfloat16),
-            pltpu.VMEM((2 * all_rows, F), jnp.bfloat16),
-            pltpu.VMEM((2, 2, TR + all_rows, TC), jnp.float32),
+            pltpu.VMEM((n_subs + 1, F, 2 * TC), jnp.bfloat16),
+            pltpu.VMEM((2, n_subs + 1, TR + all_rows, TC), jnp.float32),
             pltpu.VMEM((n_rows, 8, LANES), jnp.int32),
+            pltpu.VMEM((n_rows, 2, TR, TC), jnp.float32),
+            pltpu.VMEM((n_rows, 2, TR, TC), jnp.float32),
             pltpu.VMEM((n_rows, 2, TR, TC), jnp.bfloat16),
             pltpu.VMEM((n_rows, 2, TR, TC), jnp.bfloat16),
             pltpu.VMEM((2, TR + 2 * RAD, TC), jnp.float32),
             pltpu.VMEM((2, TR, TC), jnp.float32),
             pltpu.VMEM((2, TR, TC), jnp.float32),
-            dma((6,)),
+            dma((5 + n_subs,)),
             dma((n_rows,)),
             dma((n_rows,)),
             dma,
@@ -367,7 +369,7 @@
             dma((2, 4)),
         ],
         compiler_params=pltpu.CompilerParams(
-            collective_id=0, has_side_effects=True, vmem_limit_bytes=int(53.5 * 2**20)
+            collective_id=0, has_side_effects=True, vmem_limit_bytes=60 * 2**20
         ),
         cost_estimate=pl.CostEstimate(
             flops=8 * all_rows * depth * F, bytes_accessed=3 * 2**20, transcendentals=2**20

time: 22.9 us -> 21.7 us (0.948)
  local copies, waits for them, and re-layouts: 1.92 us -> 0 us
  Pallas kernels: 20.1 us -> 20.9 us
    unnamed x6 -> x0, local copies, waits for them, and re-layouts: 1.92 us -> none
    pallas_call x1, Pallas kernels: 18.3 us -> 19.1 us  [per_device(): form_call(owner, centres, pulses.reshape(-1, F), azimuth, table)]
where the time goes in v5:
time: 21.7 us; the launch traced here: 21.6 us
  Pallas kernels  20.9 us (96%)
  between operations  0.64 us (3%)
    pallas_call x1, Pallas kernels, per_device(): form_call(owner, centres, pulses.reshape(-1, F), azimuth, table)  19.1 us
    pallas_call x1, Pallas kernels, per_device(): last_call(form_call(owner, centres, pulses.reshape(-1, F), azimuth, table))  1.79 us

profile of v5, /device:TPU:0, one launch (start us, length us, event | category | flops | bytes accessed | tf_op | source)
XLA Modules:
  0.0 21.6 jit_solution(5435216366821595067)
XLA Ops:
  0.6 19.1 %shard_map.68.packed = f32[160,128]{1,0:T(8,128)} custom-call(s32[2]{0:T(128)} %owner_hbm.1, s32[1,1,2]{2,1,0:T(1,128)} %centres_hbm.1, bf16[512,1024]{1,0:T(8,128)(2,1)} %bitcast.1, bf16[2,256,512]{2,1,0:T(8,128)(2,1)} %constant.4.clone.azimuth_hbm, bf16[8,1024,256]{2,1,0:T(8,128)(2,1)} %constant.5.clone.table_hbm), custom_call_target="tpu_custom_call" | custom-call | flops 536870912 | bytes 3145728 | tf_op jit(solution)/shard_map/pallas_call | solution.py:403
  19.8 1.8 %shard_map.69 = (f32[32,2,128]{2,1,0:T(2,128)}, f32[32,128]{1,0:T(8,128)}) custom-call(f32[160,128]{1,0:T(8,128)} %shard_map.68.packed), custom_call_target="tpu_custom_call" | custom-call | flops 1048576 | bytes 131072 | tf_op jit(solution)/shard_map/pallas_call | solution.py:403

commit v6 on v5

--- a/solution.py
+++ b/solution.py
@@ -76,21 +76,43 @@
     return sums
 
 
-def along_cols(field, outer, sums):
+def along_cols(field, sums):
+    sums = list(sums)
+    lane = lax.broadcasted_iota(jnp.int32, (8, TC), 1)
+    centers = [field[RAD + first : RAD + first + 8, :] for first in range(0, TR, 8)]
+    for distance in range(1, RAD + 1):
+        for number, center in enumerate(centers):
+            after = jnp.where(lane < distance, OUTSIDE, center)
+            before = jnp.where(lane >= TC - distance, OUTSIDE, center)
+            nears = [
+                pltpu.roll(after, TC - distance, 1),
+                pltpu.roll(before, distance, 1),
+            ]
+            sums[number] = add(sums[number], nears, center, distance)
+    return sums
+
+
+def beside_tile(field, outer, sums):
     sums = list(sums)
     lane = lax.broadcasted_iota(jnp.int32, (8, TC), 1)
     centers = [field[RAD + first : RAD + first + 8, :] for first in range(0, TR, 8)]
     outers = [outer[first : first + 8, :] for first in range(0, TR, 8)]
     for distance in range(1, RAD + 1):
         for number, (center, outside) in enumerate(zip(centers, outers)):
-            after = jnp.where(lane < distance, outside, center)
-            before = jnp.where(lane >= TC - distance, outside, center)
-            nears = [
-                pltpu.roll(after, TC - distance, 1),
-                pltpu.roll(before, distance, 1),
-            ]
-            sums[number] = add(sums[number], nears, center, distance)
+            before = pltpu.roll(outside, distance, 1)
+            after = pltpu.roll(outside, TC - distance, 1)
+            near = jnp.where(lane >= TC - distance, after, OUTSIDE)
+            near = jnp.where(lane < distance, before, near)
+            sums[number] = add(sums[number], [near], center, distance)
     return sums
+
+
+def inside_tile(field):
+    return along_cols(field, along_rows(field, begin(field), True))
+
+
+def outside_tile(field, outer, sums):
+    return beside_tile(field, outer, along_rows(field, sums, False))
 
 
 def ratio(sums):
@@ -104,9 +126,11 @@
     save_image.start()
     field = packed.at[2 * TR : 4 * TR]
     outer = packed[4 * TR : 5 * TR, :]
-    sums = along_rows(field, begin(field), True)
-    sums = along_rows(field, sums, False)
-    sums = along_cols(field, outer, sums)
+    sums = [
+        (packed[first : first + 8, :], packed[TR + first : TR + first + 8, :])
+        for first in range(5 * TR, 6 * TR, 8)
+    ]
+    sums = outside_tile(field, outer, sums)
     despeckled[...] = ratio(sums) * (1.0 / UNIT)
     save = pltpu.make_async_copy(despeckled, despeckled_hbm, sems.at[1])
     save.start()
@@ -316,19 +340,21 @@
         packed_ref[0:TR, :] = image[0]
         packed_ref[TR : 2 * TR, :] = image[1]
         first = fields.at[0]
-        sums = along_rows(first, begin(first), True)
+        sums = inside_tile(first)
         arrive(arriving)
-        sums = along_rows(first, sums, False)
         outer = jnp.where(line < RAD, rights[0], lefts[0])
-        field = ratio(along_cols(first, outer, sums))
+        field = ratio(outside_tile(first, outer, sums))
 
         arriving = exchange(1, field)
+        for number, (top, bottom) in enumerate(inside_tile(fields.at[1])):
+            packed_ref[5 * TR + 8 * number : 5 * TR + 8 * number + 8, :] = top
+            packed_ref[6 * TR + 8 * number : 6 * TR + 8 * number + 8, :] = bottom
         to_other.wait_send()
         for copy in shift_copies + row_copies:
             copy.wait_send()
         arrive(arriving)
         packed_ref[2 * TR : 4 * TR, :] = fields[1]
-        packed_ref[4 * TR :, :] = jnp.where(line < RAD, rights[1], lefts[1])
+        packed_ref[4 * TR : 5 * TR, :] = jnp.where(line < RAD, rights[1], lefts[1])
         for sends, copy in sent:
 
             @pl.when(sends)
@@ -340,7 +366,7 @@
     hbm = pl.BlockSpec(memory_space=pltpu.HBM)
     form_call = pl.pallas_call(
         kernel,
-        out_shape=jax.ShapeDtypeStruct((5 * TR, TC), jnp.float32),
+        out_shape=jax.ShapeDtypeStruct((7 * TR, TC), jnp.float32),
         in_specs=[hbm] * 5,
         out_specs=vmem,
         scratch_shapes=[

time: 21.7 us -> 21.7 us (level)
  no operation moved by 1% of the time
where the time goes in v6:
time: 21.7 us; the launch traced here: 21.5 us
  Pallas kernels  20.9 us (96%)
  between operations  0.64 us (3%)
    pallas_call x1, Pallas kernels, per_device(): form_call(owner, centres, pulses.reshape(-1, F), azimuth, table)  19.2 us
    pallas_call x1, Pallas kernels, per_device(): last_call(form_call(owner, centres, pulses.reshape(-1, F), azimuth, table))  1.74 us

profile of v6, /device:TPU:0, one launch (start us, length us, event | category | flops | bytes accessed | tf_op | source)
XLA Modules:
  0.0 21.5 jit_solution(11245657429990287917)
XLA Ops:
  0.6 19.2 %shard_map.68.packed = f32[224,128]{1,0:T(8,128)} custom-call(s32[2]{0:T(128)} %owner_hbm.1, s32[1,1,2]{2,1,0:T(1,128)} %centres_hbm.1, bf16[512,1024]{1,0:T(8,128)(2,1)} %bitcast.1, bf16[2,256,512]{2,1,0:T(8,128)(2,1)} %constant.4.clone.azimuth_hbm, bf16[8,1024,256]{2,1,0:T(8,128)(2,1)} %constant.5.clone.table_hbm), custom_call_target="tpu_custom_call" | custom-call | flops 536870912 | bytes 3145728 | tf_op jit(solution)/shard_map/pallas_call | solution.py:429
  19.8 1.7 %shard_map.69 = (f32[32,2,128]{2,1,0:T(2,128)}, f32[32,128]{1,0:T(8,128)}) custom-call(f32[224,128]{1,0:T(8,128)} %shard_map.68.packed), custom_call_target="tpu_custom_call" | custom-call | flops 1048576 | bytes 131072 | tf_op jit(solution)/shard_map/pallas_call | solution.py:429
